TPU v7x, 256 devices: a whole 4x4x8 slice. The times are simulated.
256 devices in a mesh: tm: 32 (over z_hi, x, core), head: 8 (over z_lo, y).
Axes of the slice: x: 4, y: 4, z: 8 (z_hi: 4, z_lo: 2; z = z_hi * 2 + z_lo), core: 2. Of those that a mesh axis runs over, the one named last changes fastest.
Arguments:
- query_rows: bfloat16 [3, 16384, 4096], P(None, ('tm', 'head')), may hold values from -6 to 6
- key_rows: bfloat16 [3, 16384, 4096], P(None, ('tm', 'head')), may hold values from -6 to 6
- value_rows: bfloat16 [3, 16384, 4096], P(None, ('tm', 'head')), may hold values from -6 to 6
- step_rates: bfloat16 [3, 16384, 24], P(None, ('tm', 'head')), may hold values from 0.00048828125 to 0.005859375
- start_weights: float32 [32, 8, 3, 512, 512], P('tm', 'head'), may hold values from -0.25 to 0.25
Outputs:
- outputs: bfloat16 [3, 16384, 4096], P(None, ('tm', 'head'))
- final_weights: float32 [32, 8, 3, 512, 512], P('tm', 'head')
All inputs are finite; a program needn't handle non-finite values.
Results may differ from a plain program's by a relative error of at most 0.04.
Values may be sent and summed in bfloat16 or wider, within the bound.
No kernel may reach another device: no remote copies, remote signals or barrier semaphores. Data moves between devices by JAX's collectives and lax.ppermute only.
A program may use at most 128 MiB of HBM per device.

v0:
```python
import jax
import jax.numpy as jnp
from jax import lax
from jax.sharding import PartitionSpec as P


def passed_along(block, axis, distance):
    devices = range(lax.axis_size(axis))
    route = [(i - distance, i) for i in devices if i - distance in devices]
    return lax.ppermute(block, axis, route)


def swish_parts(inputs):
    sigmoid_value = jax.nn.sigmoid(inputs)
    return (inputs * sigmoid_value, sigmoid_value)


def contract_rows(left, right):
    return lax.dot_general(
        left, right, (((0,), (0,)), ((), ())), preferred_element_type=jnp.float32
    )


def apply_head(rounded, query_block):
    gate_part = jnp.dot(query_block, rounded[0], preferred_element_type=jnp.float32)
    up_part = jnp.dot(query_block, rounded[1], preferred_element_type=jnp.float32)
    hidden = (swish_parts(gate_part)[0] * up_part).astype(jnp.bfloat16)
    return jnp.dot(hidden, rounded[2], preferred_element_type=jnp.float32).astype(jnp.bfloat16)


def update_head(weights, rounded, key_block, value_block, rate_block):
    pre_gate = jnp.dot(key_block, rounded[0], preferred_element_type=jnp.float32)
    pre_up = jnp.dot(key_block, rounded[1], preferred_element_type=jnp.float32)
    activated, sigmoid_value = swish_parts(pre_gate)
    hidden = (activated * pre_up).astype(jnp.bfloat16)
    upstream = lax.dot_general(
        value_block, rounded[2], (((1,), (1,)), ((), ())), preferred_element_type=jnp.float32
    )
    rate_values = rate_block.astype(jnp.float32)
    gate_error = (
        rate_values[:, 0:1]
        * upstream
        * pre_up
        * sigmoid_value
        * (1.0 + pre_gate * (1.0 - sigmoid_value))
    ).astype(jnp.bfloat16)
    up_error = (rate_values[:, 1:2] * upstream * activated).astype(jnp.bfloat16)
    out_error = (rate_values[:, 2:3] * value_block.astype(jnp.float32)).astype(jnp.bfloat16)
    increment = jnp.stack(
        [
            contract_rows(key_block, gate_error),
            contract_rows(key_block, up_error),
            contract_rows(hidden, out_error),
        ]
    )
    return weights + increment


def split_heads(merged, head_count):
    return merged.reshape(merged.shape[0], head_count, merged.shape[1] // head_count)


def on_device(query_rows, key_rows, value_rows, step_rates, start_weights):
    initial = start_weights[0]
    head_count = initial.shape[0]
    tick_count = query_rows.shape[0]
    first_block = lax.axis_index("tm") == 0
    heads_apply = jax.vmap(apply_head, in_axes=(0, 1), out_axes=1)
    heads_update = jax.vmap(update_head, in_axes=(0, 0, 1, 1, 1))
    weights = initial
    last_weights = initial
    emitted = []
    for tick_index in range(tick_count):
        pieces = (
            lax.all_to_all(query_rows[tick_index], "head", split_axis=1, concat_axis=0, tiled=True),
            lax.all_to_all(key_rows[tick_index], "head", split_axis=1, concat_axis=0, tiled=True),
            lax.all_to_all(value_rows[tick_index], "head", split_axis=1, concat_axis=0, tiled=True),
            lax.all_to_all(step_rates[tick_index], "head", split_axis=1, concat_axis=0, tiled=True),
        )
        query_heads = split_heads(pieces[0], head_count)
        key_heads = split_heads(pieces[1], head_count)
        value_heads = split_heads(pieces[2], head_count)
        rate_heads = split_heads(pieces[3], head_count)
        rounded = weights.astype(jnp.bfloat16)
        produced = heads_apply(rounded, query_heads)
        produced = produced.reshape(produced.shape[0], produced.shape[1] * produced.shape[2])
        fresh_weights = heads_update(weights, rounded, key_heads, value_heads, rate_heads)
        if tick_index + 1 < tick_count:
            weights = jnp.where(first_block, initial, passed_along(fresh_weights, "tm", 1))
        else:
            last_weights = fresh_weights
        emitted.append(lax.all_to_all(produced, "head", split_axis=0, concat_axis=1, tiled=True))
    result = jnp.stack(emitted)
    return (result, last_weights[None])


def solution(mesh):
    return jax.shard_map(
        on_device,
        mesh=mesh,
        in_specs=(
            P(None, ("tm", "head"), None),
            P(None, ("tm", "head"), None),
            P(None, ("tm", "head"), None),
            P(None, ("tm", "head"), None),
            P("tm", "head", None, None, None),
        ),
        out_specs=(P(None, ("tm", "head"), None), P("tm", "head", None, None, None)),
        check_vma=False,
    )
```

profile of v0, /device:TPU:167, one launch (start us, length us, event | category | flops | bytes accessed | tf_op | source)
XLA Modules:
  0.0 351.0 jit_solution(7868348461492900468)
XLA Ops:
  2.0 5.4 %all-to-all-start.2 = ((bf16[64,8,3]{0,2,1:T(4,128)(2,1)}), bf16[64,8,3]{0,2,1:T(4,128)(2,1)S(1)}, u32[]{:S(2)}, u32[]{:S(2)}) async-start(bf16[64,8,3]{0,2,1:T(4,128)(2,1)} %all_to_all.180), calls=%async_computation.2 | async-start | bytes 16384 | tf_op jit(solution)/shard_map/all_to_all | solution.py:78
  11.2 5.2 %all-to-all-start.4 = ((bf16[64,8,512]{2,0,1:T(8,128)(2,1)}), bf16[64,8,512]{2,0,1:T(8,128)(2,1)}, u32[]{:S(2)}, u32[]{:S(2)}) async-start(bf16[64,8,512]{2,0,1:T(8,128)(2,1)} %copy.83), calls=%async_computation.4 | async-start | bytes 1048576 | tf_op jit(solution)/shard_map/all_to_all | solution.py:76
  23.5 4.8 %all-to-all-start.3 = ((bf16[64,8,512]{2,0,1:T(8,128)(2,1)}), bf16[64,8,512]{2,0,1:T(8,128)(2,1)}, u32[]{:S(2)}, u32[]{:S(2)}) async-start(bf16[64,8,512]{2,0,1:T(8,128)(2,1)} %copy.82), calls=%async_computation.3 | async-start | bytes 1048576 | tf_op jit(solution)/shard_map/all_to_all | solution.py:77
  28.4 2.7 fusion.50
  44.4 6.9 %collective-permute-start = (f32[1,3,512,512]{2,3,1,0:T(8,128)}, f32[1,3,512,512]{2,3,1,0:T(8,128)}, u32[]{:S(2)}, u32[]{:S(2)}) collective-permute-start(f32[1,3,512,512]{2,3,1,0:T(8,128)} %fusion), channel_id=1, source_target_pairs={{0,8},{8,16},{16,24},{24,32},{32,40},{40,48},{48,56},{56,64},{64,7... | collective-permute-start | bytes 9437192 | tf_op jit(solution)/shard_map/ppermute | solution.py:10
  51.9 4.0 %all-to-all-start.7 = ((bf16[64,8,3]{0,2,1:T(4,128)(2,1)}), bf16[64,8,3]{0,2,1:T(4,128)(2,1)S(1)}, u32[]{:S(2)}, u32[]{:S(2)}) async-start(bf16[64,8,3]{0,2,1:T(4,128)(2,1)} %all_to_all.194), calls=%async_computation.7 | async-start | bytes 16384 | tf_op jit(solution)/shard_map/all_to_all | solution.py:78
  56.5 70.6 %all-to-all-done.7 = bf16[64,8,3]{0,2,1:T(4,128)(2,1)S(1)} async-done(((bf16[64,8,3]{0,2,1:T(4,128)(2,1)}), bf16[64,8,3]{0,2,1:T(4,128)(2,1)S(1)}, u32[]{:S(2)}, u32[]{:S(2)}) %all-to-all-start.7) | async-done | bytes 3104 | tf_op jit(solution)/shard_map/all_to_all | solution.py:78
  127.1 4.4 %all-to-all-start.12 = ((bf16[64,8,3]{0,2,1:T(4,128)(2,1)}), bf16[64,8,3]{0,2,1:T(4,128)(2,1)S(1)}, u32[]{:S(2)}, u32[]{:S(2)}) async-start(bf16[64,8,3]{0,2,1:T(4,128)(2,1)} %all_to_all.208), calls=%async_computation.12 | async-start | bytes 16384 | tf_op jit(solution)/shard_map/all_to_all | solution.py:78
  135.7 5.0 %all-to-all-start.9 = ((bf16[64,8,512]{2,0,1:T(8,128)(2,1)}), bf16[64,8,512]{2,0,1:T(8,128)(2,1)}, u32[]{:S(2)}, u32[]{:S(2)}) async-start(bf16[64,8,512]{2,0,1:T(8,128)(2,1)} %copy.92), calls=%async_computation.9 | async-start | bytes 1048576 | tf_op jit(solution)/shard_map/all_to_all | solution.py:76
  142.8 4.3 %all-to-all-done.9 = bf16[64,8,512]{2,0,1:T(8,128)(2,1)} async-done(((bf16[64,8,512]{2,0,1:T(8,128)(2,1)}), bf16[64,8,512]{2,0,1:T(8,128)(2,1)}, u32[]{:S(2)}, u32[]{:S(2)}) %all-to-all-start.9) | async-done | bytes 524320 | tf_op jit(solution)/shard_map/all_to_all | solution.py:76
  147.2 4.8 %all-to-all-start.8 = ((bf16[64,8,512]{2,0,1:T(8,128)(2,1)}), bf16[64,8,512]{2,0,1:T(8,128)(2,1)}, u32[]{:S(2)}, u32[]{:S(2)}) async-start(bf16[64,8,512]{2,0,1:T(8,128)(2,1)} %copy.90), calls=%async_computation.8 | async-start | bytes 1048576 | tf_op jit(solution)/shard_map/all_to_all | solution.py:77
  159.2 5.2 %all-to-all-start = ((bf16[64,8,512]{2,0,1:T(8,128)(2,1)}), bf16[64,8,512]{2,0,1:T(8,128)(2,1)}, u32[]{:S(2)}, u32[]{:S(2)}) async-start(bf16[64,8,512]{2,0,1:T(8,128)(2,1)} %copy.78), calls=%async_computation | async-start | bytes 1048576 | tf_op jit(solution)/shard_map/all_to_all | solution.py:75
  171.6 2.7 convolution_bitcast_fusion.7
  174.4 5.1 %all-to-all-start.5 = ((bf16[64,8,512]{2,0,1:T(8,128)(2,1)}), bf16[64,8,512]{2,0,1:T(8,128)(2,1)}, u32[]{:S(2)}, u32[]{:S(2)}) async-start(bf16[64,8,512]{2,0,1:T(8,128)(2,1)} %copy.85), calls=%async_computation.5 | async-start | bytes 1048576 | tf_op jit(solution)/shard_map/all_to_all | solution.py:75
  181.3 2.7 convolution_bitcast_fusion.8
  184.0 2.9 convolution_bitcast_fusion.9
  186.9 5.1 %all-to-all-start.14 = ((bf16[64,8,512]{2,0,1:T(8,128)(2,1)}), bf16[64,8,512]{2,0,1:T(8,128)(2,1)}, u32[]{:S(2)}, u32[]{:S(2)}) async-start(bf16[64,8,512]{2,0,1:T(8,128)(2,1)} %copy.104), calls=%async_computation.14 | async-start | bytes 1048576 | tf_op jit(solution)/shard_map/all_to_all | solution.py:76
  192.0 5.7 %fusion.1 = f32[1,3,512,512]{2,3,1,0:T(8,128)} fusion(f32[1,1,512,512]{2,3,0,1:T(8,128)} %convolution_bitcast_fusion.7, f32[1,1,512,512]{2,3,0,1:T(8,128)} %convolution_bitcast_fusion.8, f32[1,1,512,512]{2,3,0,1:T(8,128)} %convolution_bitcast_fusion.9, f32[1,3,512,512]{2,3,1,0:T(8,128)} %collective-permute-done, f32[1,1,3,512,512]{3,4,2,1,0:T(8,128)S(1)} %copy.79, ...), kind=kLoop, calls=%fused_computation.3 | loop fusion | flops 3145728 | bytes 12582913 | tf_op jit(solution)/shard_map/vmap()/add | solution.py:56
  199.6 2.7 fusion.51
  202.3 3.3 convolution_convert_fusion.2
  205.6 5.1 %all-to-all-start.1 = ((bf16[8,64,512]{2,1,0:T(8,128)(2,1)}), bf16[8,64,512]{2,1,0:T(8,128)(2,1)}, u32[]{:S(2)}, u32[]{:S(2)}) async-start(bf16[8,64,512]{2,1,0:T(8,128)(2,1)} %bitcast.281), calls=%async_computation.1 | async-start | bytes 1048576 | tf_op jit(solution)/shard_map/all_to_all | solution.py:92
  213.4 3.3 convolution_convert_fusion.1
  216.6 64.9 %all-to-all-done.1 = bf16[8,64,512]{2,1,0:T(8,128)(2,1)} async-done(((bf16[8,64,512]{2,1,0:T(8,128)(2,1)}), bf16[8,64,512]{2,1,0:T(8,128)(2,1)}, u32[]{:S(2)}, u32[]{:S(2)}) %all-to-all-start.1) | async-done | bytes 524320 | tf_op jit(solution)/shard_map/all_to_all | solution.py:92
  281.6 4.1 %all-to-all-start.6 = ((bf16[8,64,512]{2,1,0:T(8,128)(2,1)}), bf16[8,64,512]{2,1,0:T(8,128)(2,1)}, u32[]{:S(2)}, u32[]{:S(2)}) async-start(bf16[8,64,512]{2,1,0:T(8,128)(2,1)} %bitcast.282), calls=%async_computation.6 | async-start | bytes 1048576 | tf_op jit(solution)/shard_map/all_to_all | solution.py:92
  287.8 3.6 %all-to-all-done.6 = bf16[8,64,512]{2,1,0:T(8,128)(2,1)} async-done(((bf16[8,64,512]{2,1,0:T(8,128)(2,1)}), bf16[8,64,512]{2,1,0:T(8,128)(2,1)}, u32[]{:S(2)}, u32[]{:S(2)}) %all-to-all-start.6) | async-done | bytes 524320 | tf_op jit(solution)/shard_map/all_to_all | solution.py:92
  291.5 4.8 %all-to-all-start.13 = ((bf16[64,8,512]{2,0,1:T(8,128)(2,1)}), bf16[64,8,512]{2,0,1:T(8,128)(2,1)}, u32[]{:S(2)}, u32[]{:S(2)}) async-start(bf16[64,8,512]{2,0,1:T(8,128)(2,1)} %copy.102), calls=%async_computation.13 | async-start | bytes 1048576 | tf_op jit(solution)/shard_map/all_to_all | solution.py:77
  307.0 5.2 %all-to-all-start.10 = ((bf16[64,8,512]{2,0,1:T(8,128)(2,1)}), bf16[64,8,512]{2,0,1:T(8,128)(2,1)}, u32[]{:S(2)}, u32[]{:S(2)}) async-start(bf16[64,8,512]{2,0,1:T(8,128)(2,1)} %copy.97), calls=%async_computation.10 | async-start | bytes 1048576 | tf_op jit(solution)/shard_map/all_to_all | solution.py:75
  314.6 2.9 convolution_bitcast_fusion.3
  325.1 3.3 convolution_convert_fusion
  328.4 5.1 %all-to-all-start.11 = ((bf16[8,64,512]{2,1,0:T(8,128)(2,1)}), bf16[8,64,512]{2,1,0:T(8,128)(2,1)}, u32[]{:S(2)}, u32[]{:S(2)}) async-start(bf16[8,64,512]{2,1,0:T(8,128)(2,1)} %bitcast.280), calls=%async_computation.11 | async-start | bytes 1048576 | tf_op jit(solution)/shard_map/all_to_all | solution.py:92
  339.8 4.7 %fusion.3 = f32[1,1,3,512,512]{3,4,2,1,0:T(8,128)} fusion(f32[1,1,512,512]{2,3,0,1:T(8,128)S(1)} %convolution_bitcast_fusion, f32[1,1,512,512]{2,3,0,1:T(8,128)S(1)} %convolution_bitcast_fusion.1, f32[1,1,512,512]{2,3,0,1:T(8,128)S(1)} %convolution_bitcast_fusion.2, f32[1,3,512,512]{2,3,1,0:T(8,128)} %collective-permute-done.1, ...), kind=kLoop, calls=%fused_computation.6 | loop fusion | flops 3145728 | bytes 12582913 | tf_op jit(solution)/shard_map/broadcast_in_dim | solution.py:94
  344.5 3.5 %copy.109 = f32[1,1,3,512,512]{4,3,2,1,0:T(8,128)} copy(f32[1,1,3,512,512]{3,4,2,1,0:T(8,128)} %fusion.3) | data formatting | bytes 6291456
  (110 shorter events, 85.9 us)
Async XLA Ops:
  2.0 9.2 %all-to-all-start.2 = ((bf16[64,8,3]{0,2,1:T(4,128)(2,1)}), bf16[64,8,3]{0,2,1:T(4,128)(2,1)S(1)}, u32[]{:S(2)}, u32[]{:S(2)}) async-start(bf16[64,8,3]{0,2,1:T(4,128)(2,1)} %all_to_all.180), calls=%async_computation.2 | async-start | bytes 16384 | tf_op jit(solution)/shard_map/all_to_all | solution.py:78
  9.8 6.6 %copy-start.6 = (bf16[3,64,4096]{2,1,0:T(8,128)(2,1)S(1)}, bf16[3,64,4096]{2,1,0:T(8,128)(2,1)}, u32[]{:S(2)}) copy-start(bf16[3,64,4096]{2,1,0:T(8,128)(2,1)} %param.7) | copy-start | bytes 4718596
  11.2 12.3 %all-to-all-start.4 = ((bf16[64,8,512]{2,0,1:T(8,128)(2,1)}), bf16[64,8,512]{2,0,1:T(8,128)(2,1)}, u32[]{:S(2)}, u32[]{:S(2)}) async-start(bf16[64,8,512]{2,0,1:T(8,128)(2,1)} %copy.83), calls=%async_computation.4 | async-start | bytes 1048576 | tf_op jit(solution)/shard_map/all_to_all | solution.py:76
  23.5 11.4 %all-to-all-start.3 = ((bf16[64,8,512]{2,0,1:T(8,128)(2,1)}), bf16[64,8,512]{2,0,1:T(8,128)(2,1)}, u32[]{:S(2)}, u32[]{:S(2)}) async-start(bf16[64,8,512]{2,0,1:T(8,128)(2,1)} %copy.82), calls=%async_computation.3 | async-start | bytes 1048576 | tf_op jit(solution)/shard_map/all_to_all | solution.py:77
  34.9 1.8 copy-start.14
  34.9 1.9 copy-start.15
  44.4 119.9 %collective-permute-start = (f32[1,3,512,512]{2,3,1,0:T(8,128)}, f32[1,3,512,512]{2,3,1,0:T(8,128)}, u32[]{:S(2)}, u32[]{:S(2)}) collective-permute-start(f32[1,3,512,512]{2,3,1,0:T(8,128)} %fusion), channel_id=1, source_target_pairs={{0,8},{8,16},{16,24},{24,32},{32,40},{40,48},{48,56},{56,64},{64,7... | collective-permute-start | bytes 9437192 | tf_op jit(solution)/shard_map/ppermute | solution.py:10
  51.9 75.2 %all-to-all-start.7 = ((bf16[64,8,3]{0,2,1:T(4,128)(2,1)}), bf16[64,8,3]{0,2,1:T(4,128)(2,1)S(1)}, u32[]{:S(2)}, u32[]{:S(2)}) async-start(bf16[64,8,3]{0,2,1:T(4,128)(2,1)} %all_to_all.194), calls=%async_computation.7 | async-start | bytes 16384 | tf_op jit(solution)/shard_map/all_to_all | solution.py:78
  127.1 8.5 %all-to-all-start.12 = ((bf16[64,8,3]{0,2,1:T(4,128)(2,1)}), bf16[64,8,3]{0,2,1:T(4,128)(2,1)S(1)}, u32[]{:S(2)}, u32[]{:S(2)}) async-start(bf16[64,8,3]{0,2,1:T(4,128)(2,1)} %all_to_all.208), calls=%async_computation.12 | async-start | bytes 16384 | tf_op jit(solution)/shard_map/all_to_all | solution.py:78
  135.7 11.5 %all-to-all-start.9 = ((bf16[64,8,512]{2,0,1:T(8,128)(2,1)}), bf16[64,8,512]{2,0,1:T(8,128)(2,1)}, u32[]{:S(2)}, u32[]{:S(2)}) async-start(bf16[64,8,512]{2,0,1:T(8,128)(2,1)} %copy.92), calls=%async_computation.9 | async-start | bytes 1048576 | tf_op jit(solution)/shard_map/all_to_all | solution.py:76
  147.2 12.0 %all-to-all-start.8 = ((bf16[64,8,512]{2,0,1:T(8,128)(2,1)}), bf16[64,8,512]{2,0,1:T(8,128)(2,1)}, u32[]{:S(2)}, u32[]{:S(2)}) async-start(bf16[64,8,512]{2,0,1:T(8,128)(2,1)} %copy.90), calls=%async_computation.8 | async-start | bytes 1048576 | tf_op jit(solution)/shard_map/all_to_all | solution.py:77
  154.5 2.2 copy-start.5
  155.8 2.1 copy-start.2
  159.2 15.2 %all-to-all-start = ((bf16[64,8,512]{2,0,1:T(8,128)(2,1)}), bf16[64,8,512]{2,0,1:T(8,128)(2,1)}, u32[]{:S(2)}, u32[]{:S(2)}) async-start(bf16[64,8,512]{2,0,1:T(8,128)(2,1)} %copy.78), calls=%async_computation | async-start | bytes 1048576 | tf_op jit(solution)/shard_map/all_to_all | solution.py:75
  166.8 3.8 %copy-start = (bf16[1,3,512,512]{2,3,1,0:T(8,128)(2,1)}, bf16[1,3,512,512]{2,3,1,0:T(8,128)(2,1)S(1)}, u32[]{:S(2)}) copy-start(bf16[1,3,512,512]{2,3,1,0:T(8,128)(2,1)S(1)} %fusion.4) | copy-start | bytes 4718596
  168.7 1.9 copy-start.10
  174.4 12.5 %all-to-all-start.5 = ((bf16[64,8,512]{2,0,1:T(8,128)(2,1)}), bf16[64,8,512]{2,0,1:T(8,128)(2,1)}, u32[]{:S(2)}, u32[]{:S(2)}) async-start(bf16[64,8,512]{2,0,1:T(8,128)(2,1)} %copy.85), calls=%async_computation.5 | async-start | bytes 1048576 | tf_op jit(solution)/shard_map/all_to_all | solution.py:75
  179.5 1.7 copy-start.11
  181.2 2.7 copy-start.13
  186.9 18.7 %all-to-all-start.14 = ((bf16[64,8,512]{2,0,1:T(8,128)(2,1)}), bf16[64,8,512]{2,0,1:T(8,128)(2,1)}, u32[]{:S(2)}, u32[]{:S(2)}) async-start(bf16[64,8,512]{2,0,1:T(8,128)(2,1)} %copy.104), calls=%async_computation.14 | async-start | bytes 1048576 | tf_op jit(solution)/shard_map/all_to_all | solution.py:76
  197.7 114.5 %collective-permute-start.1 = (f32[1,3,512,512]{2,3,1,0:T(8,128)}, f32[1,3,512,512]{2,3,1,0:T(8,128)}, u32[]{:S(2)}, u32[]{:S(2)}) collective-permute-start(f32[1,3,512,512]{2,3,1,0:T(8,128)} %fusion.1), channel_id=1, source_target_pairs={{0,8},{8,16},{16,24},{24,32},{32,40},{40,48},{48,56},{56,64},{64,7... | collective-permute-start | bytes 9437192 | tf_op jit(solution)/shard_map/ppermute | solution.py:10
  205.6 76.0 %all-to-all-start.1 = ((bf16[8,64,512]{2,1,0:T(8,128)(2,1)}), bf16[8,64,512]{2,1,0:T(8,128)(2,1)}, u32[]{:S(2)}, u32[]{:S(2)}) async-start(bf16[8,64,512]{2,1,0:T(8,128)(2,1)} %bitcast.281), calls=%async_computation.1 | async-start | bytes 1048576 | tf_op jit(solution)/shard_map/all_to_all | solution.py:92
  281.6 9.9 %all-to-all-start.6 = ((bf16[8,64,512]{2,1,0:T(8,128)(2,1)}), bf16[8,64,512]{2,1,0:T(8,128)(2,1)}, u32[]{:S(2)}, u32[]{:S(2)}) async-start(bf16[8,64,512]{2,1,0:T(8,128)(2,1)} %bitcast.282), calls=%async_computation.6 | async-start | bytes 1048576 | tf_op jit(solution)/shard_map/all_to_all | solution.py:92
  291.5 15.6 %all-to-all-start.13 = ((bf16[64,8,512]{2,0,1:T(8,128)(2,1)}), bf16[64,8,512]{2,0,1:T(8,128)(2,1)}, u32[]{:S(2)}, u32[]{:S(2)}) async-start(bf16[64,8,512]{2,0,1:T(8,128)(2,1)} %copy.102), calls=%async_computation.13 | async-start | bytes 1048576 | tf_op jit(solution)/shard_map/all_to_all | solution.py:77
  307.0 15.4 %all-to-all-start.10 = ((bf16[64,8,512]{2,0,1:T(8,128)(2,1)}), bf16[64,8,512]{2,0,1:T(8,128)(2,1)}, u32[]{:S(2)}, u32[]{:S(2)}) async-start(bf16[64,8,512]{2,0,1:T(8,128)(2,1)} %copy.97), calls=%async_computation.10 | async-start | bytes 1048576 | tf_op jit(solution)/shard_map/all_to_all | solution.py:75
  314.6 5.4 %copy-start.1 = (bf16[1,3,512,512]{2,3,1,0:T(8,128)(2,1)}, bf16[1,3,512,512]{2,3,1,0:T(8,128)(2,1)S(1)}, u32[]{:S(2)}) copy-start(bf16[1,3,512,512]{2,3,1,0:T(8,128)(2,1)S(1)} %fusion.5) | copy-start | bytes 4718596
  328.4 19.6 %all-to-all-start.11 = ((bf16[8,64,512]{2,1,0:T(8,128)(2,1)}), bf16[8,64,512]{2,1,0:T(8,128)(2,1)}, u32[]{:S(2)}, u32[]{:S(2)}) async-start(bf16[8,64,512]{2,1,0:T(8,128)(2,1)} %bitcast.280), calls=%async_computation.11 | async-start | bytes 1048576 | tf_op jit(solution)/shard_map/all_to_all | solution.py:92
  333.6 2.5 copy-start.7
  333.6 2.5 copy-start.8
  336.1 1.8 copy-start.9
  348.0 1.7 copy-start.3
  348.0 1.7 copy-start.4
  (1 other events, 1.1 us)
where the time goes:
time: 354 us; the launch traced here: 351 us
  waiting for transfers between devices  148 us (42%)
  starting transfers between devices  82.2 us (23%)
  matrix products  57.9 us (16%)
  local copies, waits for them, and re-layouts  41.8 us (12%)
  other arithmetic  20.3 us (6%)
    all_to_all x3, waiting for transfers between devices, on_device(): lax.all_to_all(step_rates[tick_index], 'head', split_axis=1, concat_axis=...  72.8 us
    all_to_all x3, waiting for transfers between devices, on_device(): lax.all_to_all(produced, 'head', split_axis=0, concat_axis=1, tiled=True)  68.6 us
    dot_general x9, matrix products, contract_rows(): lax.dot_general(left, right, (((0,), (0,)), ((), ())), preferred_element_...  19.7 us
    all_to_all x3, starting transfers between devices, on_device(): lax.all_to_all(query_rows[tick_index], 'head', split_axis=1, concat_axis=...  15.5 us
    all_to_all x3, starting transfers between devices, on_device(): lax.all_to_all(key_rows[tick_index], 'head', split_axis=1, concat_axis=0,...  15.4 us
    all_to_all x3, starting transfers between devices, on_device(): lax.all_to_all(value_rows[tick_index], 'head', split_axis=1, concat_axis=...  14.4 us
    all_to_all x3, starting transfers between devices, on_device(): lax.all_to_all(produced, 'head', split_axis=0, concat_axis=1, tiled=True)  14.4 us
    unnamed x43, local copies, waits for them, and re-layouts  13.9 us
  transfers between devices with their start and end apart: 17, of which 8 were waited for; matrix products, arithmetic and copies ran while one was open for 28% of the time, Pallas kernels for 0%

commit v1 on v0

v1 whole, which is shorter than its diff:
```python
import functools

import jax
import jax.numpy as jnp
from jax import lax
from jax.experimental import pallas as pl
from jax.experimental.pallas import tpu as pltpu
from jax.sharding import PartitionSpec as P

HEADS = 8
ROWS = 64
WIDTH = 512
TOKENS = HEADS * ROWS
RATE_ROWS = 16
HALF = TOKENS // 2
F32 = jnp.float32
BF16 = jnp.bfloat16
MIB = 1024 * 1024
HBM = pl.BlockSpec(memory_space=pltpu.HBM)


def run_copies(pairs, sems):
    copies = [pltpu.make_async_copy(src, dst, sems.at[i]) for i, (src, dst) in enumerate(pairs)]
    for copy in copies:
        copy.start()
    return copies


def wait_all(copies):
    for copy in copies:
        copy.wait()


def head_columns(head):
    return pl.ds(head * WIDTH, WIDTH)


def slot(index):
    return pl.ds(index * ROWS, ROWS)


def pack_first(keys, values, rates, sent, staged, rate_rows, rate_sent, load, store):
    loads = run_copies([(keys.at[0], staged.at[0]), (values.at[0], staged.at[1])], load)
    rate_rows[...] = jnp.zeros_like(rate_rows)
    for tick in range(3):
        turned = rates[tick].astype(F32).T
        for head in range(HEADS):
            rate_rows[head, 3 * tick : 3 * tick + 3, 0:ROWS] = turned[3 * head : 3 * head + 3, :]
    rate_sent[...] = rate_rows[...].astype(BF16)
    stores = run_copies([(rate_sent, sent.at[:, pl.ds(2 * ROWS, RATE_ROWS), :])], store)
    for place in range(2):
        loads[place].wait()
        for head in range(HEADS):
            copy = pltpu.make_async_copy(
                staged.at[place, :, head_columns(head)],
                sent.at[head, slot(place), :],
                store.at[1 + place * HEADS + head],
            )
            copy.start()
            stores.append(copy)
    wait_all(stores)


def send_first(keys, values, rates):
    return pl.pallas_call(
        pack_first,
        out_shape=pltpu.HBM((HEADS, 2 * ROWS + RATE_ROWS, WIDTH), BF16),
        in_specs=[HBM, HBM, pl.BlockSpec(memory_space=pltpu.VMEM)],
        out_specs=HBM,
        scratch_shapes=[
            pltpu.VMEM((2, ROWS, HEADS * WIDTH), BF16),
            pltpu.VMEM((HEADS, RATE_ROWS, WIDTH), F32),
            pltpu.VMEM((HEADS, RATE_ROWS, WIDTH), BF16),
            pltpu.SemaphoreType.DMA((2,)),
            pltpu.SemaphoreType.DMA((2 * HEADS + 1,)),
        ],
        cost_estimate=pl.CostEstimate(flops=0, bytes_accessed=2 * MIB, transcendentals=0),
        name="pack_first",
    )(keys, values, rates)


def pack_rest(queries, keys, values, second, third, staged, load, store):
    plan = (
        (second, 0, keys, 1),
        (second, 1, values, 1),
        (third, 0, keys, 2),
        (third, 1, values, 2),
        (third, 2, queries, 0),
        (third, 3, queries, 1),
        (third, 4, queries, 2),
    )
    loads = run_copies([(source.at[tick], staged.at[i]) for i, (_, _, source, tick) in enumerate(plan)], load)
    stores = []
    for i, (target, place, _, _) in enumerate(plan):
        loads[i].wait()
        for head in range(HEADS):
            copy = pltpu.make_async_copy(
                staged.at[i, :, head_columns(head)], target.at[head, slot(place), :], store.at[i * HEADS + head]
            )
            copy.start()
            stores.append(copy)
    wait_all(stores)


def send_rest(queries, keys, values):
    return pl.pallas_call(
        pack_rest,
        out_shape=(
            pltpu.HBM((HEADS, 2 * ROWS, WIDTH), BF16),
            pltpu.HBM((HEADS, 5 * ROWS, WIDTH), BF16),
        ),
        in_specs=[HBM] * 3,
        out_specs=(HBM, HBM),
        scratch_shapes=[
            pltpu.VMEM((7, ROWS, HEADS * WIDTH), BF16),
            pltpu.SemaphoreType.DMA((7,)),
            pltpu.SemaphoreType.DMA((7 * HEADS,)),
        ],
        cost_estimate=pl.CostEstimate(flops=0, bytes_accessed=7 * MIB, transcendentals=0),
        name="pack_rest",
    )(queries, keys, values)


def unpack_outputs(received, result, staged, load, store):
    loads = run_copies(
        [
            (received.at[head, slot(tick), :], staged.at[tick, :, head_columns(head)])
            for tick in range(3)
            for head in range(HEADS)
        ],
        load,
    )
    stores = []
    for tick in range(3):
        wait_all(loads[tick * HEADS : (tick + 1) * HEADS])
        copy = pltpu.make_async_copy(staged.at[tick], result.at[tick], store.at[tick])
        copy.start()
        stores.append(copy)
    wait_all(stores)


def place_outputs(received):
    return pl.pallas_call(
        unpack_outputs,
        out_shape=pltpu.HBM((3, ROWS, HEADS * WIDTH), BF16),
        in_specs=[HBM],
        out_specs=HBM,
        scratch_shapes=[
            pltpu.VMEM((3, ROWS, HEADS * WIDTH), BF16),
            pltpu.SemaphoreType.DMA((3 * HEADS,)),
            pltpu.SemaphoreType.DMA((3,)),
        ],
        cost_estimate=pl.CostEstimate(flops=0, bytes_accessed=3 * MIB, transcendentals=0),
        name="unpack_outputs",
    )(received)


def dot(left, right, left_dim=1, right_dim=0):
    return lax.dot_general(left, right, (((left_dim,), (right_dim,)), ((), ())), preferred_element_type=F32)


def rate_columns(rates, tick, first_source, sources):
    parts = []
    for source in range(first_source, first_source + sources):
        turned = rates[source, :, 0:128].astype(F32).T
        parts.append(turned[0:ROWS, 3 * tick : 3 * tick + 3])
    return jnp.concatenate(parts, axis=0)


def errors_of(rounded, pair, rates, tick, work):
    gate_error, up_error, hidden, out_error = work
    for half in range(2):
        sources = pl.ds(half * 4, 4)
        rows = pl.ds(half * HALF, HALF)
        keys = pair[sources, 0:ROWS, :].reshape(HALF, WIDTH)
        values = pair[sources, ROWS : 2 * ROWS, :].reshape(HALF, WIDTH)
        rate = rate_columns(rates, tick, half * 4, 4)
        pre_gate = dot(keys, rounded[0])
        pre_up = dot(keys, rounded[1])
        upstream = dot(values, rounded[2], 1, 1)
        sigmoid_value = jax.nn.sigmoid(pre_gate)
        activated = pre_gate * sigmoid_value
        hidden[rows, :] = (activated * pre_up).astype(BF16)
        gate_error[rows, :] = (
            rate[:, 0:1] * upstream * pre_up * sigmoid_value * (1.0 + pre_gate * (1.0 - sigmoid_value))
        ).astype(BF16)
        up_error[rows, :] = (rate[:, 1:2] * upstream * activated).astype(BF16)
        out_error[rows, :] = (rate[:, 2:3] * values.astype(F32)).astype(BF16)


def write_updates(added, pair, work, fresh, out, sems):
    gate_error, up_error, hidden, out_error = work
    copies = []
    for half in range(2):
        columns = pl.ds(half * HALF, HALF)
        keys = pair[:, 0:ROWS, columns].reshape(TOKENS, HALF)
        steps = (
            (keys, gate_error),
            (keys, up_error),
            (hidden[:, columns], out_error),
        )
        for index, (left, right) in enumerate(steps):
            value = added[index, columns, :].astype(F32) + dot(left, right[...], 0, 0)
            fresh[index, columns, :] = value.astype(fresh.dtype)
            copy = pltpu.make_async_copy(
                fresh.at[index, columns, :], out.at[index, columns, :], sems.at[half * 3 + index]
            )
            copy.start()
            copies.append(copy)
    wait_all(copies)


WORK = [pltpu.VMEM((TOKENS, WIDTH), BF16)] * 4


def start_update(start, received, out, pair, wide, rounded, fresh, e0, e1, hid, e2, sems, load):
    copies = run_copies([(received, pair), (start, wide)], load)
    wait_all(copies)
    rounded[...] = wide[...].astype(BF16)
    work = (e0, e1, hid, e2)
    errors_of(rounded, pair.at[:, 0 : 2 * ROWS, :], pair.at[:, 2 * ROWS :, :], 0, work)
    write_updates(wide, pair, work, fresh, out, sems)


def update_start(start, received):
    return pl.pallas_call(
        start_update,
        out_shape=pltpu.HBM((3, WIDTH, WIDTH), BF16),
        in_specs=[HBM, HBM],
        out_specs=HBM,
        scratch_shapes=[
            pltpu.VMEM((HEADS, 2 * ROWS + RATE_ROWS, WIDTH), BF16),
            pltpu.VMEM((3, WIDTH, WIDTH), F32),
            pltpu.VMEM((3, WIDTH, WIDTH), BF16),
            pltpu.VMEM((3, WIDTH, WIDTH), BF16),
            *WORK,
            pltpu.SemaphoreType.DMA((6,)),
            pltpu.SemaphoreType.DMA((2,)),
        ],
        compiler_params=pltpu.CompilerParams(vmem_limit_bytes=40 * MIB),
        cost_estimate=pl.CostEstimate(flops=0, bytes_accessed=0, transcendentals=0),
        name="update_start",
    )(start, received)


def fetch_weights(start, from_core, from_chip, rounded, load):
    place = lax.axis_index("tm")
    odd = lax.rem(place, 2) == 1
    if from_core is not None:

        @pl.when(odd)
        def _():
            copy = pltpu.make_async_copy(from_core, rounded, load)
            copy.start()
            copy.wait()

    if from_chip is not None:

        @pl.when(jnp.logical_and(jnp.logical_not(odd), place > 0))
        def _():
            copy = pltpu.make_async_copy(from_chip, rounded, load)
            copy.start()
            copy.wait()

        @pl.when(place == 0)
        def _():
            def with_start(wide):
                copy = pltpu.make_async_copy(start, wide, load)
                copy.start()
                copy.wait()
                rounded[...] = wide[...].astype(BF16)

            pl.run_scoped(with_start, pltpu.VMEM((3, WIDTH, WIDTH), F32))


def later_update(cores, tick, *refs):
    refs = list(refs)
    start = refs.pop(0)
    from_core = refs.pop(0) if cores in (1, None) else None
    from_chip = refs.pop(0) if cores in (0, None) else None
    received, first, out, pair, rates, rounded, fresh, e0, e1, hid, e2, sems, load = refs

    def run():
        copies = run_copies(
            [
                (received.at[:, pl.ds(0, 2 * ROWS), :], pair),
                (first.at[:, pl.ds(2 * ROWS, RATE_ROWS), :], rates),
            ],
            load,
        )
        fetch_weights(start, from_core, from_chip, rounded, load.at[2])
        wait_all(copies)
        work = (e0, e1, hid, e2)
        errors_of(rounded, pair, rates, tick, work)
        write_updates(rounded, pair, work, fresh, out, sems)

    if cores is None:
        run()
    else:
        pl.when(lax.rem(lax.axis_index("tm"), 2) == cores)(run)


def update_later(cores, tick, kind, start, weights, received, first):
    operands = [start, *weights, received, first]
    return pl.pallas_call(
        functools.partial(later_update, cores, tick),
        out_shape=pltpu.HBM((3, WIDTH, WIDTH), kind),
        in_specs=[HBM] * len(operands),
        out_specs=HBM,
        scratch_shapes=[
            pltpu.VMEM((HEADS, 2 * ROWS, WIDTH), BF16),
            pltpu.VMEM((HEADS, RATE_ROWS, WIDTH), BF16),
            pltpu.VMEM((3, WIDTH, WIDTH), BF16),
            pltpu.VMEM((3, WIDTH, WIDTH), kind),
            *WORK,
            pltpu.SemaphoreType.DMA((6,)),
            pltpu.SemaphoreType.DMA((3,)),
        ],
        compiler_params=pltpu.CompilerParams(vmem_limit_bytes=40 * MIB),
        cost_estimate=pl.CostEstimate(flops=0, bytes_accessed=0, transcendentals=0),
        name="update_tick%d_%s" % (tick, {0: "even", 1: "odd", None: "all"}[cores]),
    )(*operands)


def apply_weights(rounded, query, produced):
    for half in range(2):
        sources = pl.ds(half * 4, 4)
        queries = query[sources, :, :].reshape(HALF, WIDTH)
        gate_part = dot(queries, rounded[0])
        up_part = dot(queries, rounded[1])
        hidden = (gate_part * jax.nn.sigmoid(gate_part) * up_part).astype(BF16)
        produced[sources, :, :] = dot(hidden, rounded[2]).astype(BF16).reshape(4, ROWS, WIDTH)


def early_apply(start, from_core, from_chip, received, out, query, wide, rounded, produced, sems):
    copies = run_copies(
        [
            (received.at[:, slot(2), :], query.at[0]),
            (received.at[:, slot(3), :], query.at[1]),
            (start, wide),
        ],
        sems,
    )
    wait_all(copies)
    rounded[...] = wide[...].astype(BF16)
    apply_weights(rounded, query.at[0], produced.at[0])
    first = pltpu.make_async_copy(produced.at[0], out.at[:, slot(0), :], sems.at[0])
    first.start()
    fetch_weights(start, from_core, from_chip, rounded, sems.at[2])
    apply_weights(rounded, query.at[1], produced.at[1])
    second = pltpu.make_async_copy(produced.at[1], out.at[:, slot(1), :], sems.at[1])
    second.start()
    first.wait()
    second.wait()


def apply_early(start, from_core, from_chip, received):
    return pl.pallas_call(
        early_apply,
        out_shape=pltpu.HBM((HEADS, 3 * ROWS, WIDTH), BF16),
        in_specs=[HBM] * 4,
        out_specs=HBM,
        scratch_shapes=[
            pltpu.VMEM((2, HEADS, ROWS, WIDTH), BF16),
            pltpu.VMEM((3, WIDTH, WIDTH), F32),
            pltpu.VMEM((3, WIDTH, WIDTH), BF16),
            pltpu.VMEM((2, HEADS, ROWS, WIDTH), BF16),
            pltpu.SemaphoreType.DMA((3,)),
        ],
        compiler_params=pltpu.CompilerParams(vmem_limit_bytes=40 * MIB),
        cost_estimate=pl.CostEstimate(flops=0, bytes_accessed=0, transcendentals=0),
        name="apply_ticks01",
    )(start, from_core, from_chip, received)


def late_apply(start, from_core, from_chip, received, held, out, query, rounded, produced, sems):
    del held
    copy = pltpu.make_async_copy(received.at[:, slot(4), :], query, sems.at[0])
    copy.start()
    fetch_weights(start, from_core, from_chip, rounded, sems.at[1])
    copy.wait()
    apply_weights(rounded, query, produced)
    last = pltpu.make_async_copy(produced, out.at[:, slot(2), :], sems.at[0])
    last.start()
    last.wait()


def apply_late(start, from_core, from_chip, received, held):
    return pl.pallas_call(
        late_apply,
        out_shape=pltpu.HBM((HEADS, 3 * ROWS, WIDTH), BF16),
        in_specs=[HBM] * 5,
        out_specs=HBM,
        scratch_shapes=[
            pltpu.VMEM((HEADS, ROWS, WIDTH), BF16),
            pltpu.VMEM((3, WIDTH, WIDTH), BF16),
            pltpu.VMEM((HEADS, ROWS, WIDTH), BF16),
            pltpu.SemaphoreType.DMA((2,)),
        ],
        input_output_aliases={4: 0},
        compiler_params=pltpu.CompilerParams(vmem_limit_bytes=40 * MIB),
        cost_estimate=pl.CostEstimate(flops=0, bytes_accessed=0, transcendentals=0),
        name="apply_tick2",
    )(start, from_core, from_chip, received, held)


def exchange(block):
    return lax.all_to_all(block, "head", split_axis=0, concat_axis=0, tiled=True)


def after(*arrays):
    return lax.optimization_barrier(arrays)


def on_device(query_rows, key_rows, value_rows, step_rates, start_weights):
    start = start_weights[0, 0]
    places = lax.axis_size("tm")
    to_core = [(i, i + 1) for i in range(0, places, 2)]
    to_chip = [(i, i + 1) for i in range(1, places - 1, 2)]

    first_sent = send_first(key_rows, value_rows, step_rates)
    first = exchange(first_sent)
    query_rows, key_rows, value_rows, _ = after(query_rows, key_rows, value_rows, first_sent)
    second_sent, third_sent = send_rest(query_rows, key_rows, value_rows)
    fresh0 = update_start(start, first)
    core1 = lax.ppermute(fresh0, "tm", to_core)
    chip1 = lax.ppermute(fresh0, "tm", to_chip)
    second_sent, _ = after(second_sent, fresh0)
    second = exchange(second_sent)
    fresh1_odd = update_later(1, 1, BF16, start, [core1], second, first)
    third_sent, chip1, _ = after(third_sent, chip1, fresh1_odd)
    third = exchange(third_sent)
    fresh1_even = update_later(0, 1, BF16, start, [chip1], second, first)
    core2 = lax.ppermute(fresh1_even, "tm", to_core)
    chip2 = lax.ppermute(fresh1_odd, "tm", to_chip)
    third, _ = after(third, fresh1_even)
    held = apply_early(start, core1, chip1, third)
    held = apply_late(start, core2, chip2, third, held)
    returned = exchange(held)
    final = update_later(None, 2, F32, start, [core2, chip2], third, first)
    return place_outputs(returned), final[None, None]


def solution(mesh):
    return jax.shard_map(
        on_device,
        mesh=mesh,
        in_specs=(
            P(None, ("tm", "head"), None),
            P(None, ("tm", "head"), None),
            P(None, ("tm", "head"), None),
            P(None, ("tm", "head"), None),
            P("tm", "head", None, None, None),
        ),
        out_specs=(P(None, ("tm", "head"), None), P("tm", "head", None, None, None)),
        check_vma=False,
    )
```

time: 354 us -> 180 us (0.51)
  the two profiles are of different devices: /device:TPU:167 before, /device:TPU:160 now
where the time goes in v1:
time: 180 us; the launch traced here: 178 us
  waiting for transfers between devices  77.2 us (43%)
  starting transfers between devices  62.1 us (34%)
  Pallas kernels  32.7 us (18%)
  local copies, waits for them, and re-layouts  5.4 us (3%)
    all_to_all x4, starting transfers between devices, exchange(): lax.all_to_all(block, 'head', split_axis=0, concat_axis=0, tiled=True)  55.6 us
    all_to_all x4, waiting for transfers between devices, exchange(): lax.all_to_all(block, 'head', split_axis=0, concat_axis=0, tiled=True)  38.9 us
    ppermute x1, waiting for transfers between devices, on_device(): chip1 = lax.ppermute(fresh0, 'tm', to_chip)  24 us
    ppermute x1, waiting for transfers between devices, on_device(): chip2 = lax.ppermute(fresh1_odd, 'tm', to_chip)  12.4 us
    pallas_call x3, Pallas kernels, update_later(): pl.pallas_call(functools.partial(later_update, cores, tick), out_shape=pl...  9.93 us
    pallas_call x1, Pallas kernels, apply_early(): pl.pallas_call(early_apply, out_shape=pltpu.HBM((HEADS, 3 * ROWS, WIDTH),...  5.96 us
    unnamed x9, local copies, waits for them, and re-layouts  5.4 us
    pallas_call x1, Pallas kernels, update_start(): pl.pallas_call(start_update, out_shape=pltpu.HBM((3, WIDTH, WIDTH), BF16)...  4.28 us
  transfers between devices with their start and end apart: 8, of which 7 were waited for; matrix products, arithmetic and copies ran while one was open for 0% of the time, Pallas kernels for 11%

profile of v1, /device:TPU:160, one launch (start us, length us, event | category | flops | bytes accessed | tf_op | source)
XLA Modules:
  0.0 178.1 jit_solution(6611361005078692643)
XLA Ops:
  0.6 1.4 copy.8.rates
  2.1 3.0 %pack_first.1 = bf16[8,144,512]{2,1,0:T(8,128)(2,1)} custom-call(bf16[3,64,4096]{2,1,0:T(8,128)(2,1)} %keys.2, bf16[3,64,4096]{2,1,0:T(8,128)(2,1)} %values.2, bf16[3,64,24]{2,1,0:T(8,128)(2,1)} %copy.8.rates), custom_call_target="tpu_custom_call" | custom-call | bytes 2097152 | tf_op jit(solution)/shard_map/pack_first/pallas_call | solution.py:65
  5.1 5.9 %all-to-all-start = ((bf16[8,144,512]{2,1,0:T(8,128)(2,1)}), bf16[8,144,512]{2,1,0:T(8,128)(2,1)}, u32[]{:S(2)}, u32[]{:S(2)}) async-start(bf16[8,144,512]{2,1,0:T(8,128)(2,1)} %pack_first.1), calls=%async_computation | async-start | bytes 2359296 | tf_op jit(solution)/shard_map/all_to_all | solution.py:408
  11.0 3.6 %pack_rest.1 = (bf16[8,128,512]{2,1,0:T(8,128)(2,1)}, bf16[8,320,512]{2,1,0:T(8,128)(2,1)}) custom-call(bf16[3,64,4096]{2,1,0:T(8,128)(2,1)} %queries, bf16[3,64,4096]{2,1,0:T(8,128)(2,1)} %keys.2, bf16[3,64,4096]{2,1,0:T(8,128)(2,1)} %values.2), custom_call_target="tpu_custom_call" | custom-call | bytes 7340032 | tf_op jit(solution)/shard_map/pack_rest/pallas_call | solution.py:106
  14.6 12.2 %all-to-all-done.received.refs_3_.refs_4_ = bf16[8,144,512]{2,1,0:T(8,128)(2,1)} async-done(((bf16[8,144,512]{2,1,0:T(8,128)(2,1)}), bf16[8,144,512]{2,1,0:T(8,128)(2,1)}, u32[]{:S(2)}, u32[]{:S(2)}) %all-to-all-start) | async-done | bytes 1179680 | tf_op jit(solution)/shard_map/all_to_all | solution.py:408
  26.8 0.0 copy-done
  26.8 4.3 %update_start.1 = bf16[3,512,512]{2,1,0:T(8,128)(2,1)} custom-call(f32[3,512,512]{2,1,0:T(8,128)S(1)} %bitcast.2, bf16[8,144,512]{2,1,0:T(8,128)(2,1)} %all-to-all-done.received.refs_3_.refs_4_), custom_call_target="tpu_custom_call" | custom-call | tf_op jit(solution)/shard_map/update_start/pallas_call | solution.py:226
  31.0 4.7 %all-to-all-start.1 = ((bf16[8,128,512]{2,1,0:T(8,128)(2,1)}), bf16[8,128,512]{2,1,0:T(8,128)(2,1)}, u32[]{:S(2)}, u32[]{:S(2)}) async-start(bf16[8,128,512]{2,1,0:T(8,128)(2,1)} %get-tuple-element.16), calls=%async_computation.1 | async-start | bytes 2097152 | tf_op jit(solution)/shard_map/all_to_all | solution.py:408
  35.8 1.4 collective-permute-start.1
  37.1 1.3 collective-permute-start
  38.4 1.8 %collective-permute-done.1.refs_1_.from_core = bf16[3,512,512]{2,1,0:T(8,128)(2,1)S(1)} collective-permute-done((bf16[3,512,512]{2,1,0:T(8,128)(2,1)}, bf16[3,512,512]{2,1,0:T(8,128)(2,1)S(1)}, u32[]{:S(2)}, u32[]{:S(2)}) %collective-permute-start.1) | collective-permute-done | bytes 1572896 | tf_op jit(solution)/shard_map/ppermute | solution.py:426
  40.3 0.0 copy-start.1
  40.3 1.1 copy-done.1
  41.4 8.8 %all-to-all-done.1.refs_2_ = bf16[8,128,512]{2,1,0:T(8,128)(2,1)} async-done(((bf16[8,128,512]{2,1,0:T(8,128)(2,1)}), bf16[8,128,512]{2,1,0:T(8,128)(2,1)}, u32[]{:S(2)}, u32[]{:S(2)}) %all-to-all-start.1) | async-done | bytes 1048608 | tf_op jit(solution)/shard_map/all_to_all | solution.py:408
  50.2 0.0 copy-start.2
  50.2 1.4 copy-done.2
  51.6 0.1 update_tick1_odd.1
  51.7 24.0 %collective-permute-done.refs_1_.from_chip = bf16[3,512,512]{2,1,0:T(8,128)(2,1)} collective-permute-done((bf16[3,512,512]{2,1,0:T(8,128)(2,1)}, bf16[3,512,512]{2,1,0:T(8,128)(2,1)}, u32[]{:S(2)}, u32[]{:S(2)}) %collective-permute-start) | collective-permute-done | bytes 1572896 | tf_op jit(solution)/shard_map/ppermute | solution.py:427
  75.8 17.9 %all-to-all-start.2 = ((bf16[8,320,512]{2,1,0:T(8,128)(2,1)}), bf16[8,320,512]{2,1,0:T(8,128)(2,1)}, u32[]{:S(2)}, u32[]{:S(2)}) async-start(bf16[8,320,512]{2,1,0:T(8,128)(2,1)} %get-tuple-element.18), calls=%async_computation.2 | async-start | bytes 5242880 | tf_op jit(solution)/shard_map/all_to_all | solution.py:408
  93.7 4.8 %update_tick1_even.1 = bf16[3,512,512]{2,1,0:T(8,128)(2,1)} custom-call(f32[3,512,512]{2,1,0:T(8,128)S(1)} %bitcast.4, bf16[3,512,512]{2,1,0:T(8,128)(2,1)} %collective-permute-done.refs_1_.from_chip, bf16[8,128,512]{2,1,0:T(8,128)(2,1)} %all-to-all-done.1.refs_2_, bf16[8,144,512]{2,1,0:T(8,128)(2,1)} %all-to-all-done.received.refs_3_.refs_4_), custom_call_target="tpu_custom_call" | custom-call | tf_op jit(solution)/shard_map/update_tick1_even/pallas_call | solution.py:305
  98.5 2.5 %collective-permute-start.2 = (bf16[3,512,512]{2,1,0:T(8,128)(2,1)}, bf16[3,512,512]{2,1,0:T(8,128)(2,1)}, u32[]{:S(2)}, u32[]{:S(2)}) collective-permute-start(bf16[3,512,512]{2,1,0:T(8,128)(2,1)} %update_tick1_even.1), channel_id=1, source_target_pairs={{0,8},{16,24},{32,40},{48,56},{64,72},{80,88},{96,104},{112,120},{... | collective-permute-start | bytes 4718600 | tf_op jit(solution)/shard_map/ppermute | solution.py:434
  100.9 1.3 collective-permute-start.3
  102.2 10.0 %all-to-all-done.2.received.refs_3_ = bf16[8,320,512]{2,1,0:T(8,128)(2,1)} async-done(((bf16[8,320,512]{2,1,0:T(8,128)(2,1)}), bf16[8,320,512]{2,1,0:T(8,128)(2,1)}, u32[]{:S(2)}, u32[]{:S(2)}) %all-to-all-start.2) | async-done | bytes 2621472 | tf_op jit(solution)/shard_map/all_to_all | solution.py:408
  112.2 1.4 copy-done.3
  113.6 6.0 %apply_ticks01.1.held = bf16[8,192,512]{2,1,0:T(8,128)(2,1)} custom-call(f32[3,512,512]{2,1,0:T(8,128)S(1)} %bitcast.5, bf16[3,512,512]{2,1,0:T(8,128)(2,1)S(1)} %copy-done.3, bf16[3,512,512]{2,1,0:T(8,128)(2,1)} %collective-permute-done.refs_1_.from_chip, bf16[8,320,512]{2,1,0:T(8,128)(2,1)} %all-to-all-done.2.received.refs_3_), custom_call_target="tpu_custom_call" | custom-call | tf_op jit(solution)/shard_map/apply_ticks01/pallas_call | solution.py:358
  119.6 0.0 collective-permute-done.2.from_core.refs_1_
  119.6 12.4 %collective-permute-done.3.from_chip.refs_2_ = bf16[3,512,512]{2,1,0:T(8,128)(2,1)} collective-permute-done((bf16[3,512,512]{2,1,0:T(8,128)(2,1)}, bf16[3,512,512]{2,1,0:T(8,128)(2,1)}, u32[]{:S(2)}, u32[]{:S(2)}) %collective-permute-start.3) | collective-permute-done | bytes 1572896 | tf_op jit(solution)/shard_map/ppermute | solution.py:435
  132.1 3.5 %apply_tick2.1 = bf16[8,192,512]{2,1,0:T(8,128)(2,1)} custom-call(f32[3,512,512]{2,1,0:T(8,128)S(1)} %bitcast.6, bf16[3,512,512]{2,1,0:T(8,128)(2,1)} %collective-permute-done.2.from_core.refs_1_, bf16[3,512,512]{2,1,0:T(8,128)(2,1)} %collective-permute-done.3.from_chip.refs_2_, ...), custom_call_target="tpu_custom_call", output_to_operand_aliasing={{}: (4, {})} | custom-call | tf_op jit(solution)/shard_map/apply_tick2/pallas_call | solution.py:389
  135.6 27.1 %all-to-all-start.3 = ((bf16[8,192,512]{2,1,0:T(8,128)(2,1)}), bf16[8,192,512]{2,1,0:T(8,128)(2,1)}, u32[]{:S(2)}, u32[]{:S(2)}) async-start(bf16[8,192,512]{2,1,0:T(8,128)(2,1)} %apply_tick2.1), calls=%async_computation.3 | async-start | bytes 3145728 | tf_op jit(solution)/shard_map/all_to_all | solution.py:408
  162.7 5.1 %update_tick2_all.1 = f32[3,512,512]{2,1,0:T(8,128)} custom-call(f32[3,512,512]{2,1,0:T(8,128)S(1)} %bitcast.7, bf16[3,512,512]{2,1,0:T(8,128)(2,1)} %collective-permute-done.2.from_core.refs_1_, bf16[3,512,512]{2,1,0:T(8,128)(2,1)} %collective-permute-done.3.from_chip.refs_2_, bf16[8,320,512]{2,1,0:T(8,128)(2,1)} %all-to-all-done.2.received.refs_3_, ...), custom_call_target="tpu_custom_call" | custom-call | tf_op jit(solution)/shard_map/update_tick2_all/pallas_call | solution.py:305
  167.7 7.9 %all-to-all-done.3.received = bf16[8,192,512]{2,1,0:T(8,128)(2,1)} async-done(((bf16[8,192,512]{2,1,0:T(8,128)(2,1)}), bf16[8,192,512]{2,1,0:T(8,128)(2,1)}, u32[]{:S(2)}, u32[]{:S(2)}) %all-to-all-start.3) | async-done | bytes 1572896 | tf_op jit(solution)/shard_map/all_to_all | solution.py:408
  175.6 2.4 %unpack_outputs.1 = bf16[3,64,4096]{2,1,0:T(8,128)(2,1)} custom-call(bf16[8,192,512]{2,1,0:T(8,128)(2,1)} %all-to-all-done.3.received), custom_call_target="tpu_custom_call" | custom-call | bytes 3145728 | tf_op jit(solution)/shard_map/unpack_outputs/pallas_call | solution.py:143
  (2 shorter events, 0.0 us)
Async XLA Ops:
  5.1 21.7 %all-to-all-start = ((bf16[8,144,512]{2,1,0:T(8,128)(2,1)}), bf16[8,144,512]{2,1,0:T(8,128)(2,1)}, u32[]{:S(2)}, u32[]{:S(2)}) async-start(bf16[8,144,512]{2,1,0:T(8,128)(2,1)} %pack_first.1), calls=%async_computation | async-start | bytes 2359296 | tf_op jit(solution)/shard_map/all_to_all | solution.py:408
  11.0 15.8 %copy-start = (f32[1,1,3,512,512]{4,3,2,1,0:T(8,128)S(1)}, f32[1,1,3,512,512]{4,3,2,1,0:T(8,128)}, u32[]{:S(2)}) copy-start(f32[1,1,3,512,512]{4,3,2,1,0:T(8,128)} %param.9) | copy-start | bytes 9437188
  31.0 19.2 %all-to-all-start.1 = ((bf16[8,128,512]{2,1,0:T(8,128)(2,1)}), bf16[8,128,512]{2,1,0:T(8,128)(2,1)}, u32[]{:S(2)}, u32[]{:S(2)}) async-start(bf16[8,128,512]{2,1,0:T(8,128)(2,1)} %get-tuple-element.16), calls=%async_computation.1 | async-start | bytes 2097152 | tf_op jit(solution)/shard_map/all_to_all | solution.py:408
  35.8 4.5 %collective-permute-start.1 = (bf16[3,512,512]{2,1,0:T(8,128)(2,1)}, bf16[3,512,512]{2,1,0:T(8,128)(2,1)S(1)}, u32[]{:S(2)}, u32[]{:S(2)}) collective-permute-start(bf16[3,512,512]{2,1,0:T(8,128)(2,1)} %update_start.1), channel_id=1, source_target_pairs={{0,8},{16,24},{32,40},{48,56},{64,72},{80,88},{96,104},{112,120},{... | collective-permute-start | bytes 4718600 | tf_op jit(solution)/shard_map/ppermute | solution.py:426
  37.1 38.6 %collective-permute-start = (bf16[3,512,512]{2,1,0:T(8,128)(2,1)}, bf16[3,512,512]{2,1,0:T(8,128)(2,1)}, u32[]{:S(2)}, u32[]{:S(2)}) collective-permute-start(bf16[3,512,512]{2,1,0:T(8,128)(2,1)} %update_start.1), channel_id=1, source_target_pairs={{8,16},{24,32},{40,48},{56,64},{72,80},{88,96},{104,112},{120,128}... | collective-permute-start | bytes 4718600 | tf_op jit(solution)/shard_map/ppermute | solution.py:427
  40.3 1.1 copy-start.1
  50.2 1.4 copy-start.2
  75.8 36.5 %all-to-all-start.2 = ((bf16[8,320,512]{2,1,0:T(8,128)(2,1)}), bf16[8,320,512]{2,1,0:T(8,128)(2,1)}, u32[]{:S(2)}, u32[]{:S(2)}) async-start(bf16[8,320,512]{2,1,0:T(8,128)(2,1)} %get-tuple-element.18), calls=%async_computation.2 | async-start | bytes 5242880 | tf_op jit(solution)/shard_map/all_to_all | solution.py:408
  98.5 21.2 %collective-permute-start.2 = (bf16[3,512,512]{2,1,0:T(8,128)(2,1)}, bf16[3,512,512]{2,1,0:T(8,128)(2,1)}, u32[]{:S(2)}, u32[]{:S(2)}) collective-permute-start(bf16[3,512,512]{2,1,0:T(8,128)(2,1)} %update_tick1_even.1), channel_id=1, source_target_pairs={{0,8},{16,24},{32,40},{48,56},{64,72},{80,88},{96,104},{112,120},{... | collective-permute-start | bytes 4718600 | tf_op jit(solution)/shard_map/ppermute | solution.py:434
  100.9 31.1 %collective-permute-start.3 = (bf16[3,512,512]{2,1,0:T(8,128)(2,1)}, bf16[3,512,512]{2,1,0:T(8,128)(2,1)}, u32[]{:S(2)}, u32[]{:S(2)}) collective-permute-start(bf16[3,512,512]{2,1,0:T(8,128)(2,1)} %update_tick1_odd.1), channel_id=1, source_target_pairs={{8,16},{24,32},{40,48},{56,64},{72,80},{88,96},{104,112},{120,128}... | collective-permute-start | bytes 4718600 | tf_op jit(solution)/shard_map/ppermute | solution.py:435
  112.2 1.4 copy-start.3
  135.6 40.0 %all-to-all-start.3 = ((bf16[8,192,512]{2,1,0:T(8,128)(2,1)}), bf16[8,192,512]{2,1,0:T(8,128)(2,1)}, u32[]{:S(2)}, u32[]{:S(2)}) async-start(bf16[8,192,512]{2,1,0:T(8,128)(2,1)} %apply_tick2.1), calls=%async_computation.3 | async-start | bytes 3145728 | tf_op jit(solution)/shard_map/all_to_all | solution.py:408

commit v2 on v0

v2 whole, which is shorter than its diff:
```python
import functools

import jax
import jax.numpy as jnp
from jax import lax
from jax.experimental import pallas as pl
from jax.experimental.pallas import tpu as pltpu
from jax.sharding import PartitionSpec as P

HEADS = 8
ROWS = 64
WIDTH = 512
TOKENS = HEADS * ROWS
RATE_ROWS = 16
HALF = TOKENS // 2
F32 = jnp.float32
BF16 = jnp.bfloat16
MIB = 1024 * 1024
FREE = pl.CostEstimate(flops=0, bytes_accessed=0, transcendentals=0)
PLANE = 8
ANY = pl.BlockSpec(memory_space=pl.ANY)
HBM = pl.BlockSpec(memory_space=pltpu.HBM)


def run_copies(pairs, sems):
    copies = [pltpu.make_async_copy(src, dst, sems.at[i]) for i, (src, dst) in enumerate(pairs)]
    for copy in copies:
        copy.start()
    return copies


def wait_all(copies):
    for copy in copies:
        copy.wait()


def head_columns(head):
    return pl.ds(head * WIDTH, WIDTH)


def slot(index):
    return pl.ds(index * ROWS, ROWS)


def pack_arrays(plan, staged, load, store):
    loads = run_copies([(source.at[tick], staged.at[i]) for i, (source, tick, _, _) in enumerate(plan)], load)
    stores = []
    for i, (_, _, target, place) in enumerate(plan):
        loads[i].wait()
        for head in range(HEADS):
            copy = pltpu.make_async_copy(
                staged.at[i, :, head_columns(head)], target.at[head, slot(place), :], store.at[i * HEADS + head]
            )
            copy.start()
            stores.append(copy)
    return stores


def pack_first(keys, values, rates, sent, staged, rate_rows, rate_sent, load, store):
    plan = ((keys, 0, sent, 0), (values, 0, sent, 1), (keys, 1, sent, 2), (values, 1, sent, 3))
    stores = pack_arrays(plan, staged, load, store)
    rate_rows[...] = jnp.zeros_like(rate_rows)
    for tick in range(3):
        turned = rates[tick].astype(F32)
        for head in range(HEADS):
            rate_rows[head, 3 * tick : 3 * tick + 3, 0:ROWS] = turned[3 * head : 3 * head + 3, :]
    rate_sent[...] = rate_rows[...].astype(BF16)
    last = pltpu.make_async_copy(rate_sent, sent.at[:, pl.ds(4 * ROWS, RATE_ROWS), :], store.at[4 * HEADS])
    last.start()
    wait_all(stores)
    last.wait()


def send_first(keys, values, rates):
    return pl.pallas_call(
        pack_first,
        out_shape=pltpu.HBM((HEADS, 4 * ROWS + RATE_ROWS, WIDTH), BF16),
        in_specs=[HBM, HBM, pl.BlockSpec(memory_space=pltpu.VMEM)],
        out_specs=HBM,
        scratch_shapes=[
            pltpu.VMEM((4, ROWS, HEADS * WIDTH), BF16),
            pltpu.VMEM((HEADS, RATE_ROWS, WIDTH), F32),
            pltpu.VMEM((HEADS, RATE_ROWS, WIDTH), BF16),
            pltpu.SemaphoreType.DMA((4,)),
            pltpu.SemaphoreType.DMA((4 * HEADS + 1,)),
        ],
        cost_estimate=FREE,
        name="pack_first",
    )(keys, values, rates)


def pack_rest(queries, keys, values, sent, staged, load, store):
    plan = (
        (queries, 0, sent, 0),
        (queries, 1, sent, 1),
        (queries, 2, sent, 2),
        (keys, 2, sent, 3),
        (values, 2, sent, 4),
    )
    wait_all(pack_arrays(plan, staged, load, store))


def send_rest(queries, keys, values):
    return pl.pallas_call(
        pack_rest,
        out_shape=pltpu.HBM((HEADS, 5 * ROWS, WIDTH), BF16),
        in_specs=[HBM] * 3,
        out_specs=HBM,
        scratch_shapes=[
            pltpu.VMEM((5, ROWS, HEADS * WIDTH), BF16),
            pltpu.SemaphoreType.DMA((5,)),
            pltpu.SemaphoreType.DMA((5 * HEADS,)),
        ],
        cost_estimate=FREE,
        name="pack_rest",
    )(queries, keys, values)


def unpack_arrays(plan, staged, load, store):
    loads = run_copies(
        [
            (source.at[head, slot(place), :], staged.at[i, :, head_columns(head)])
            for i, (source, place, _, _) in enumerate(plan)
            for head in range(HEADS)
        ],
        load,
    )
    stores = []
    for i, (_, _, target, tick) in enumerate(plan):
        wait_all(loads[i * HEADS : (i + 1) * HEADS])
        copy = pltpu.make_async_copy(staged.at[i], target.at[tick], store.at[i])
        copy.start()
        stores.append(copy)
    wait_all(stores)


def unpack_outputs(received, result, staged, load, store):
    unpack_arrays([(received, tick, result, tick) for tick in range(3)], staged, load, store)


def place_outputs(received):
    return pl.pallas_call(
        unpack_outputs,
        out_shape=pltpu.HBM((3, ROWS, HEADS * WIDTH), BF16),
        in_specs=[ANY],
        out_specs=HBM,
        scratch_shapes=[
            pltpu.VMEM((3, ROWS, HEADS * WIDTH), BF16),
            pltpu.SemaphoreType.DMA((3 * HEADS,)),
            pltpu.SemaphoreType.DMA((3,)),
        ],
        cost_estimate=FREE,
        name="unpack_outputs",
    )(received)


def dot(left, right, left_dim=1, right_dim=0):
    return lax.dot_general(left, right, (((left_dim,), (right_dim,)), ((), ())), preferred_element_type=F32)


def rate_columns(rates, tick, first_source, sources):
    parts = []
    for source in range(first_source, first_source + sources):
        turned = rates[source, :, 0:128].astype(F32).T
        parts.append(turned[0:ROWS, 3 * tick : 3 * tick + 3])
    return jnp.concatenate(parts, axis=0)


def errors_of(rounded, pair, rates, tick, work):
    gate_error, up_error, hidden, out_error = work
    for half in range(2):
        sources = pl.ds(half * 4, 4)
        rows = pl.ds(half * HALF, HALF)
        keys = pair[sources, 0:ROWS, :].reshape(HALF, WIDTH)
        values = pair[sources, ROWS : 2 * ROWS, :].reshape(HALF, WIDTH)
        rate = rate_columns(rates, tick, half * 4, 4)
        pre_gate = dot(keys, rounded[0])
        pre_up = dot(keys, rounded[1])
        upstream = dot(values, rounded[2], 1, 1)
        sigmoid_value = jax.nn.sigmoid(pre_gate)
        activated = pre_gate * sigmoid_value
        hidden[rows, :] = (activated * pre_up).astype(BF16)
        gate_error[rows, :] = (
            rate[:, 0:1] * upstream * pre_up * sigmoid_value * (1.0 + pre_gate * (1.0 - sigmoid_value))
        ).astype(BF16)
        up_error[rows, :] = (rate[:, 1:2] * upstream * activated).astype(BF16)
        out_error[rows, :] = (rate[:, 2:3] * values.astype(F32)).astype(BF16)


def is_odd():
    return lax.rem(lax.axis_index("tm"), 2) == 1


STACK = (3, WIDTH, WIDTH)
PARTS = ((WIDTH, WIDTH), (2 * WIDTH, WIDTH))
TOKEN = pltpu.HBM((8, 128), F32)


def piece(parts, index, half):
    if index == 0:
        return parts[0].at[pl.ds(half * HALF, HALF), :]
    return parts[1].at[pl.ds((index - 1) * WIDTH + half * HALF, HALF), :]


def stack_piece(stack, index, half):
    return stack.at[index, pl.ds(half * HALF, HALF), :]


def write_updates(added, pair, work, fresh, routes, sems):
    gate_error, up_error, hidden, out_error = work
    started = []
    for index in (1, 2, 0):
        for half in range(2):
            columns = pl.ds(half * HALF, HALF)
            keys = pair[:, 0:ROWS, columns].reshape(TOKENS, HALF)
            left, right = ((keys, gate_error), (keys, up_error), (hidden[:, columns], out_error))[index]
            value = added[index, columns, :].astype(F32) + dot(left, right[...], 0, 0)
            fresh[index, columns, :] = value.astype(fresh.dtype)
            for predicate, target in routes:
                copy = pltpu.make_async_copy(
                    fresh.at[index, columns, :], target(index, half), sems.at[half * 3 + index]
                )
                if predicate is None:
                    copy.start()
                else:
                    pl.when(predicate)(copy.start)
                started.append((predicate, copy))
    for predicate, copy in started:
        if predicate is None:
            copy.wait()
        else:
            pl.when(predicate)(copy.wait)


WORK = [pltpu.VMEM((TOKENS, WIDTH), BF16)] * 4


def start_update(start, received, stacked, part0, part1, pair, rates, wide, rounded, fresh, e0, e1, hid, e2, sems, load):
    copies = run_copies(
        [
            (start, wide),
            (received.at[:, pl.ds(0, 2 * ROWS), :], pair),
            (received.at[:, pl.ds(4 * ROWS, RATE_ROWS), :], rates),
        ],
        load,
    )
    copies[0].wait()
    rounded[...] = wide[...].astype(BF16)
    wait_all(copies[1:])
    work = (e0, e1, hid, e2)
    errors_of(rounded, pair, rates, 0, work)
    odd = is_odd()
    routes = (
        (odd, functools.partial(piece, (part0, part1))),
        (jnp.logical_not(odd), functools.partial(stack_piece, stacked)),
    )
    write_updates(wide, pair, work, fresh, routes, sems)


def update_start(start, received):
    return pl.pallas_call(
        start_update,
        out_shape=tuple(pltpu.HBM(shape, BF16) for shape in (STACK, *PARTS)),
        in_specs=[ANY, ANY],
        out_specs=(HBM,) * 3,
        scratch_shapes=[
            pltpu.VMEM((HEADS, 2 * ROWS, WIDTH), BF16),
            pltpu.VMEM((HEADS, RATE_ROWS, WIDTH), BF16),
            pltpu.VMEM(STACK, F32),
            pltpu.VMEM(STACK, BF16),
            pltpu.VMEM(STACK, BF16),
            *WORK,
            pltpu.SemaphoreType.DMA((6,)),
            pltpu.SemaphoreType.DMA((3,)),
        ],
        compiler_params=pltpu.CompilerParams(vmem_limit_bytes=40 * MIB),
        cost_estimate=FREE,
        name="update_start",
    )(start, received)


def fetch_from_chip(start, from_chip, rounded, load):
    place = lax.axis_index("tm")
    crossed = lax.rem(place, PLANE) == 0
    direct, straight, relayed = from_chip

    def gather(parts):
        order = ((0, 0), (0, 1), (1, 0), (1, 1), (2, 0), (2, 1))
        wait_all(run_copies([(piece(parts, *which), stack_piece(rounded, *which)) for which in order], load))

    pl.when(jnp.logical_not(crossed))(lambda: gather((direct, straight)))
    pl.when(jnp.logical_and(crossed, place > 0))(lambda: gather((direct, relayed)))

    @pl.when(place == 0)
    def _():
        def with_start(wide):
            wait_all(run_copies([(start, wide)], load))
            rounded[...] = wide[...].astype(BF16)

        pl.run_scoped(with_start, pltpu.VMEM(STACK, F32))


def fetch_own(from_core, rounded, load):
    wait_all(run_copies([(from_core, rounded)], load))


def middle_update(cores, *refs):
    refs = list(refs)
    first = refs.pop(0)
    if not cores:
        refs.pop(0)
    weights = [refs.pop(0) for _ in range(1 if cores else 4)]
    used, outs = refs.pop(0), [refs.pop(0) for _ in range(1 + cores)]
    _, pair, rates, rounded, fresh, e0, e1, hid, e2, sems, load, keep = refs

    @pl.when(lax.rem(lax.axis_index("tm"), 2) == cores)
    def _():
        copies = run_copies(
            [
                (first.at[:, pl.ds(2 * ROWS, 2 * ROWS), :], pair),
                (first.at[:, pl.ds(4 * ROWS, RATE_ROWS), :], rates),
            ],
            keep,
        )
        if cores:
            fetch_own(weights[0], rounded, load)
        else:
            fetch_from_chip(weights[0], weights[1:], rounded, load)
        wait_all(copies)
        kept = pltpu.make_async_copy(rounded, used, keep.at[0])
        kept.start()
        work = (e0, e1, hid, e2)
        errors_of(rounded, pair, rates, 1, work)
        route = functools.partial(piece, outs) if cores else functools.partial(stack_piece, outs[0])
        write_updates(rounded, pair, work, fresh, ((None, route),), sems)
        kept.wait()


def update_middle(cores, first, token, weights):
    operands = [first, *weights] if cores else [first, token, *weights]
    outs = PARTS if cores else [STACK]
    return pl.pallas_call(
        functools.partial(middle_update, cores),
        out_shape=(pltpu.HBM(STACK, BF16), *[pltpu.HBM(shape, BF16) for shape in outs], TOKEN),
        in_specs=[ANY] * len(operands),
        out_specs=(*[HBM] * (1 + len(outs)), HBM),
        scratch_shapes=[
            pltpu.VMEM((HEADS, 2 * ROWS, WIDTH), BF16),
            pltpu.VMEM((HEADS, RATE_ROWS, WIDTH), BF16),
            pltpu.VMEM(STACK, BF16),
            pltpu.VMEM(STACK, BF16),
            *WORK,
            pltpu.SemaphoreType.DMA((6,)),
            pltpu.SemaphoreType.DMA((6,)),
            pltpu.SemaphoreType.DMA((2,)),
        ],
        compiler_params=pltpu.CompilerParams(vmem_limit_bytes=40 * MIB),
        cost_estimate=FREE,
        name="update_tick1_%s" % ("odd" if cores else "even"),
    )(*operands)


def last_update(used, received, first, out, pair, rates, rounded, fresh, e0, e1, hid, e2, sems, load):
    wait_all(
        run_copies(
            [
                (received.at[:, pl.ds(3 * ROWS, 2 * ROWS), :], pair),
                (first.at[:, pl.ds(4 * ROWS, RATE_ROWS), :], rates),
                (used, rounded),
            ],
            load,
        )
    )
    work = (e0, e1, hid, e2)
    errors_of(rounded, pair, rates, 2, work)
    write_updates(rounded, pair, work, fresh, ((None, functools.partial(stack_piece, out)),), sems)


def update_last(used, received, first):
    return pl.pallas_call(
        last_update,
        out_shape=pltpu.HBM(STACK, F32),
        in_specs=[ANY] * 3,
        out_specs=HBM,
        scratch_shapes=[
            pltpu.VMEM((HEADS, 2 * ROWS, WIDTH), BF16),
            pltpu.VMEM((HEADS, RATE_ROWS, WIDTH), BF16),
            pltpu.VMEM(STACK, BF16),
            pltpu.VMEM(STACK, F32),
            *WORK,
            pltpu.SemaphoreType.DMA((6,)),
            pltpu.SemaphoreType.DMA((3,)),
        ],
        compiler_params=pltpu.CompilerParams(vmem_limit_bytes=40 * MIB),
        cost_estimate=FREE,
        name="update_tick2",
    )(used, received, first)


def apply_weights(rounded, query, produced):
    for half in range(2):
        sources = pl.ds(half * 4, 4)
        queries = query[sources, :, :].reshape(HALF, WIDTH)
        gate_part = dot(queries, rounded[0])
        up_part = dot(queries, rounded[1])
        hidden = (gate_part * jax.nn.sigmoid(gate_part) * up_part).astype(BF16)
        produced[sources, :, :] = dot(hidden, rounded[2]).astype(BF16).reshape(4, ROWS, WIDTH)


def first_apply(start, received, out, _, query, wide, rounded, produced, sems):
    copies = run_copies([(start, wide), (received.at[:, slot(0), :], query)], sems)
    copies[0].wait()
    rounded[...] = wide[...].astype(BF16)
    copies[1].wait()
    apply_weights(rounded, query, produced)
    wait_all(run_copies([(produced, out.at[:, slot(0), :])], sems))


def apply_first(start, received):
    return pl.pallas_call(
        first_apply,
        out_shape=(pltpu.HBM((HEADS, 3 * ROWS, WIDTH), BF16), TOKEN),
        in_specs=[ANY] * 2,
        out_specs=(HBM, HBM),
        scratch_shapes=[
            pltpu.VMEM((HEADS, ROWS, WIDTH), BF16),
            pltpu.VMEM(STACK, F32),
            pltpu.VMEM(STACK, BF16),
            pltpu.VMEM((HEADS, ROWS, WIDTH), BF16),
            pltpu.SemaphoreType.DMA((2,)),
        ],
        compiler_params=pltpu.CompilerParams(vmem_limit_bytes=40 * MIB),
        cost_estimate=FREE,
        name="apply_tick0",
    )(start, received)


def middle_apply(used_odd, used_even, received, held, out, _, query, rounded, produced, sems):
    del held
    copies = run_copies([(received.at[:, slot(1), :], query)], sems)
    odd = is_odd()
    pl.when(odd)(lambda: fetch_own(used_odd, rounded, sems.at[pl.ds(1, 1)]))
    pl.when(jnp.logical_not(odd))(lambda: fetch_own(used_even, rounded, sems.at[pl.ds(1, 1)]))
    wait_all(copies)
    apply_weights(rounded, query, produced)
    wait_all(run_copies([(produced, out.at[:, slot(1), :])], sems))


def apply_middle(used_odd, used_even, received, held):
    return pl.pallas_call(
        middle_apply,
        out_shape=(pltpu.HBM((HEADS, 3 * ROWS, WIDTH), BF16), TOKEN),
        in_specs=[ANY] * 4,
        out_specs=(HBM, HBM),
        input_output_aliases={3: 0},
        scratch_shapes=[
            pltpu.VMEM((HEADS, ROWS, WIDTH), BF16),
            pltpu.VMEM(STACK, BF16),
            pltpu.VMEM((HEADS, ROWS, WIDTH), BF16),
            pltpu.SemaphoreType.DMA((2,)),
        ],
        compiler_params=pltpu.CompilerParams(vmem_limit_bytes=40 * MIB),
        cost_estimate=FREE,
        name="apply_tick1",
    )(used_odd, used_even, received, held)


def late_apply(token, start, from_core, direct, straight, relayed, received, held, out, used, query, rounded, produced, sems, load):
    del token, held
    copy = pltpu.make_async_copy(received.at[:, slot(2), :], query, sems.at[0])
    copy.start()
    odd = is_odd()
    pl.when(odd)(lambda: fetch_own(from_core, rounded, load))
    pl.when(jnp.logical_not(odd))(lambda: fetch_from_chip(start, (direct, straight, relayed), rounded, load))
    copy.wait()
    kept = pltpu.make_async_copy(rounded, used, sems.at[1])
    kept.start()
    apply_weights(rounded, query, produced)
    last = pltpu.make_async_copy(produced, out.at[:, slot(2), :], sems.at[0])
    last.start()
    last.wait()
    kept.wait()


def apply_late(token, start, from_core, from_chip, received, held):
    operands = (token, start, from_core, *from_chip, received, held)
    return pl.pallas_call(
        late_apply,
        out_shape=(pltpu.HBM((HEADS, 3 * ROWS, WIDTH), BF16), pltpu.HBM(STACK, BF16)),
        in_specs=[ANY] * len(operands),
        out_specs=(HBM, HBM),
        input_output_aliases={len(operands) - 1: 0},
        scratch_shapes=[
            pltpu.VMEM((HEADS, ROWS, WIDTH), BF16),
            pltpu.VMEM(STACK, BF16),
            pltpu.VMEM((HEADS, ROWS, WIDTH), BF16),
            pltpu.SemaphoreType.DMA((2,)),
            pltpu.SemaphoreType.DMA((6,)),
        ],
        compiler_params=pltpu.CompilerParams(vmem_limit_bytes=40 * MIB),
        cost_estimate=FREE,
        name="apply_tick2",
    )(*operands)


def in_hbm(array):
    return pltpu.with_memory_space_constraint(array, pltpu.HBM)


def exchange(block):
    return lax.all_to_all(block, "head", split_axis=0, concat_axis=0, tiled=True)


def after(*arrays):
    return lax.optimization_barrier(arrays)


def mark_body(first, second, out):
    del first, second, out


def mark(first, second, flops):
    return pl.pallas_call(
        mark_body,
        out_shape=TOKEN,
        in_specs=[HBM, HBM],
        out_specs=HBM,
        cost_estimate=pl.CostEstimate(flops=flops, bytes_accessed=0, transcendentals=0),
        name="mark",
    )(first, second)


def routes_of(places):
    to_core = [(i, i + 1) for i in range(0, places, 2)]
    to_chip = [(i, i + 1) for i in range(1, places - 1, 2)]
    inward, onward = [], []
    for i, j in to_chip:
        for head in range(HEADS):
            if j % PLANE:
                inward.append((i * HEADS + head, j * HEADS + head))
            else:
                relay = i - PLANE + 2 if head < HEADS // 2 else i - PLANE + 4
                inward.append((i * HEADS + head, relay * HEADS + head))
                onward.append((relay * HEADS + head, j * HEADS + head))
    return to_core, to_chip, inward, onward


def on_device(query_rows, key_rows, value_rows, step_rates, start_weights):
    start = in_hbm(start_weights[0, 0])
    to_core, to_chip, inward, onward = routes_of(lax.axis_size("tm"))

    def shift(block, route):
        return lax.ppermute(block, "tm", route)

    def relay(block, route):
        return lax.ppermute(block, ("tm", "head"), route)

    first_sent = send_first(key_rows, value_rows, jnp.swapaxes(step_rates, 1, 2))
    first = in_hbm(exchange(first_sent))
    query_rows, key_rows, value_rows, first_sent = after(query_rows, key_rows, value_rows, first_sent)
    second_sent = send_rest(query_rows, key_rows, value_rows)
    second = in_hbm(exchange(second_sent))

    stacked, part0, part1 = update_start(start, first)
    core1 = shift(stacked, to_core)
    straight1 = relay(part1, inward)
    direct1 = shift(part0, to_chip)
    used_odd, part0, part1, token = update_middle(1, first, None, [core1])
    straight2 = relay(part1, inward)
    direct2 = shift(part0, to_chip)
    straight1, token = after(straight1, token)
    relayed1 = relay(straight1, onward)
    straight2, token = after(straight2, token)
    relayed2 = relay(straight2, onward)
    direct1, token = after(direct1, token)
    relayed1, token = after(relayed1, mark(token, token, 6 * 10**9))
    used_even, stacked, token = update_middle(0, first, token, [start, direct1, straight1, relayed1])
    core2 = shift(stacked, to_core)
    second, token = after(second, token)
    held, _ = apply_first(start, second)
    held, early = apply_middle(used_odd, used_even, second, held)
    direct2, early, token = after(direct2, early, token)
    relayed2, token = after(relayed2, mark(token, early, 3 * 10**9))
    core2, token = after(core2, mark(token, token, 12 * 10**9))
    held, used2 = apply_late(token, start, core2, [direct2, straight2, relayed2], second, held)
    returned = exchange(held)
    final = update_last(used2, second, first)
    result = place_outputs(returned)
    return result, final[None, None]


def solution(mesh):
    return jax.shard_map(
        on_device,
        mesh=mesh,
        in_specs=(
            P(None, ("tm", "head"), None),
            P(None, ("tm", "head"), None),
            P(None, ("tm", "head"), None),
            P(None, ("tm", "head"), None),
            P("tm", "head", None, None, None),
        ),
        out_specs=(P(None, ("tm", "head"), None), P("tm", "head", None, None, None)),
        check_vma=False,
    )
```

time: 354 us -> 138 us (0.39)
  the two profiles are of different devices: /device:TPU:167 before, /device:TPU:160 now
where the time goes in v2:
time: 138 us; the launch traced here: 136 us
  waiting for transfers between devices  59.4 us (43%)
  starting transfers between devices  35.9 us (26%)
  Pallas kernels  33.7 us (24%)
  local copies, waits for them, and re-layouts  5.8 us (4%)
    all_to_all x3, waiting for transfers between devices, exchange(): lax.all_to_all(block, 'head', split_axis=0, concat_axis=0, tiled=True)  35.2 us
    all_to_all x3, starting transfers between devices, exchange(): lax.all_to_all(block, 'head', split_axis=0, concat_axis=0, tiled=True)  26.4 us
    ppermute x4, waiting for transfers between devices, shift(): return lax.ppermute(block, 'tm', route)  14.7 us
    ppermute x4, waiting for transfers between devices, relay(): return lax.ppermute(block, ('tm', 'head'), route)  9.51 us
    unnamed x20, local copies, waits for them, and re-layouts  5.8 us
    ppermute x4, starting transfers between devices, shift(): return lax.ppermute(block, 'tm', route)  5.36 us
    pallas_call x1, Pallas kernels, update_start(): pl.pallas_call(start_update, out_shape=tuple((pltpu.HBM(shape, BF16) for...  5.18 us
    pallas_call x1, Pallas kernels, update_last(): pl.pallas_call(last_update, out_shape=pltpu.HBM(STACK, F32), in_specs=[AN...  4.49 us
  transfers between devices with their start and end apart: 11, of which 5 were waited for; matrix products, arithmetic and copies ran while one was open for 0% of the time, Pallas kernels for 18%

profile of v2, /device:TPU:160, one launch (start us, length us, event | category | flops | bytes accessed | tf_op | source)
XLA Modules:
  0.0 135.7 jit_solution(8978263494574294057)
XLA Ops:
  0.6 3.5 %pack_first.1 = bf16[8,272,512]{2,1,0:T(8,128)(2,1)} custom-call(bf16[3,64,4096]{2,1,0:T(8,128)(2,1)} %keys.2, bf16[3,64,4096]{2,1,0:T(8,128)(2,1)} %values.2, bf16[3,24,64]{2,1,0:T(8,128)(2,1)} %bitcast.8), custom_call_target="tpu_custom_call" | custom-call | tf_op jit(solution)/shard_map/pack_first/pallas_call | solution.py:75
  4.1 5.9 %all-to-all-start = ((bf16[8,272,512]{2,1,0:T(8,128)(2,1)}), bf16[8,272,512]{2,1,0:T(8,128)(2,1)S(1)}, u32[]{:S(2)}, u32[]{:S(2)}) async-start(bf16[8,272,512]{2,1,0:T(8,128)(2,1)} %pack_first.1), calls=%async_computation | async-start | bytes 4456448 | tf_op jit(solution)/shard_map/all_to_all | solution.py:511
  10.1 2.9 %pack_rest.1 = bf16[8,320,512]{2,1,0:T(8,128)(2,1)} custom-call(bf16[3,64,4096]{2,1,0:T(8,128)(2,1)} %queries, bf16[3,64,4096]{2,1,0:T(8,128)(2,1)} %keys.2, bf16[3,64,4096]{2,1,0:T(8,128)(2,1)} %values.2), custom_call_target="tpu_custom_call" | custom-call | tf_op jit(solution)/shard_map/pack_rest/pallas_call | solution.py:104
  13.0 24.0 %all-to-all-done.received.refs_0_.first = bf16[8,272,512]{2,1,0:T(8,128)(2,1)S(1)} async-done(((bf16[8,272,512]{2,1,0:T(8,128)(2,1)}), bf16[8,272,512]{2,1,0:T(8,128)(2,1)S(1)}, u32[]{:S(2)}, u32[]{:S(2)}) %all-to-all-start) | async-done | bytes 2228256 | tf_op jit(solution)/shard_map/all_to_all | solution.py:511
  37.0 1.4 %copy-done.7 = bf16[8,272,512]{2,1,0:T(8,128)(2,1)} copy-done((bf16[8,272,512]{2,1,0:T(8,128)(2,1)}, bf16[8,272,512]{2,1,0:T(8,128)(2,1)S(1)}, u32[]{:S(2)}) %copy-start.7) | copy-done | bytes 2228248
  38.3 4.8 %all-to-all-start.1 = ((bf16[8,320,512]{2,1,0:T(8,128)(2,1)}), bf16[8,320,512]{2,1,0:T(8,128)(2,1)}, u32[]{:S(2)}, u32[]{:S(2)}) async-start(bf16[8,320,512]{2,1,0:T(8,128)(2,1)} %pack_rest.1), calls=%async_computation.1 | async-start | bytes 5242880 | tf_op jit(solution)/shard_map/all_to_all | solution.py:511
  43.2 5.2 %update_start.1 = (bf16[3,512,512]{2,1,0:T(8,128)(2,1)}, bf16[512,512]{1,0:T(8,128)(2,1)}, bf16[1024,512]{1,0:T(8,128)(2,1)}) custom-call(f32[3,512,512]{2,1,0:T(8,128)} %bitcast.3, bf16[8,272,512]{2,1,0:T(8,128)(2,1)} %copy-done.7), custom_call_target="tpu_custom_call" | custom-call | tf_op jit(solution)/shard_map/update_start/pallas_call | solution.py:261
  48.4 1.4 %collective-permute-start.1 = (bf16[3,512,512]{2,1,0:T(8,128)(2,1)}, bf16[3,512,512]{2,1,0:T(8,128)(2,1)S(1)}, u32[]{:S(2)}, u32[]{:S(2)}) collective-permute-start(bf16[3,512,512]{2,1,0:T(8,128)(2,1)} %get-tuple-element.38), channel_id=1, source_target_pairs={{0,8},{16,24},{32,40},{48,56},{64,72},{80,88},{96,104},{112,120},{... | collective-permute-start | bytes 4718600 | tf_op jit(solution)/shard_map/ppermute | solution.py:553
  49.8 0.9 collective-permute-start
  50.6 2.3 %collective-permute-done.1.refs_1_ = bf16[3,512,512]{2,1,0:T(8,128)(2,1)S(1)} collective-permute-done((bf16[3,512,512]{2,1,0:T(8,128)(2,1)}, bf16[3,512,512]{2,1,0:T(8,128)(2,1)S(1)}, u32[]{:S(2)}, u32[]{:S(2)}) %collective-permute-start.1) | collective-permute-done | bytes 1572896 | tf_op jit(solution)/shard_map/ppermute | solution.py:553
  52.9 0.1 update_tick1_odd.1
  53.0 0.7 collective-permute-start.4
  53.8 1.3 collective-permute-start.3
  55.1 1.3 collective-permute-start.2
  56.4 1.3 collective-permute-start.6
  57.7 1.3 collective-permute-start.7
  59.0 12.5 %collective-permute-done.3.refs_3_ = bf16[512,512]{1,0:T(8,128)(2,1)S(1)} collective-permute-done((bf16[512,512]{1,0:T(8,128)(2,1)S(1)}, bf16[512,512]{1,0:T(8,128)(2,1)S(1)}, u32[]{:S(2)}, u32[]{:S(2)}) %collective-permute-start.3) | collective-permute-done | bytes 524320 | tf_op jit(solution)/shard_map/ppermute | solution.py:553
  71.5 0.8 copy-done.3
  72.3 9.5 %collective-permute-done.2.refs_5_ = bf16[1024,512]{1,0:T(8,128)(2,1)S(1)} collective-permute-done((bf16[1024,512]{1,0:T(8,128)(2,1)S(1)}, bf16[1024,512]{1,0:T(8,128)(2,1)S(1)}, u32[]{:S(2)}, u32[]{:S(2)}) %collective-permute-start.2) | collective-permute-done | bytes 1048608 | tf_op jit(solution)/shard_map/ppermute | solution.py:556
  81.8 1.0 copy-done.4
  82.8 0.7 copy-done.5
  83.5 4.3 %update_tick1_even.1 = (bf16[3,512,512]{2,1,0:T(8,128)(2,1)}, bf16[3,512,512]{2,1,0:T(8,128)(2,1)}, f32[8,128]{1,0:T(8,128)}) custom-call(bf16[8,272,512]{2,1,0:T(8,128)(2,1)} %copy-done.7, f32[8,128]{1,0:T(8,128)S(1)} %copy-done.5, f32[3,512,512]{2,1,0:T(8,128)} %bitcast.4, bf16[512,512]{1,0:T(8,128)(2,1)S(1)} %copy-done.4, ...), custom_call_target="tpu_custom_call" | custom-call | tf_op jit(solution)/shard_map/update_tick1_even/pallas_call | solution.py:342
  87.8 1.4 %collective-permute-start.5 = (bf16[3,512,512]{2,1,0:T(8,128)(2,1)}, bf16[3,512,512]{2,1,0:T(8,128)(2,1)S(1)}, u32[]{:S(2)}, u32[]{:S(2)}) collective-permute-start(bf16[3,512,512]{2,1,0:T(8,128)(2,1)} %get-tuple-element.49), channel_id=1, source_target_pairs={{0,8},{16,24},{32,40},{48,56},{64,72},{80,88},{96,104},{112,120},{... | collective-permute-start | bytes 4718600 | tf_op jit(solution)/shard_map/ppermute | solution.py:553
  89.2 4.2 %apply_tick0.1 = (bf16[8,192,512]{2,1,0:T(8,128)(2,1)}, f32[8,128]{1,0:T(8,128)}) custom-call(f32[3,512,512]{2,1,0:T(8,128)} %bitcast.5, bf16[8,320,512]{2,1,0:T(8,128)(2,1)} %all-to-all-done.1.received), custom_call_target="tpu_custom_call" | custom-call | tf_op jit(solution)/shard_map/apply_tick0/pallas_call | solution.py:420
  93.5 3.0 %apply_tick1.1 = (bf16[8,192,512]{2,1,0:T(8,128)(2,1)}, f32[8,128]{1,0:T(8,128)}) custom-call(bf16[3,512,512]{2,1,0:T(8,128)(2,1)S(1)} %copy-done, bf16[3,512,512]{2,1,0:T(8,128)(2,1)S(1)} %copy-done.1, bf16[8,320,512]{2,1,0:T(8,128)(2,1)} %all-to-all-done.1.received, bf16[8,192,512]{2,1,0:T(8,128)(2,1)} %get-tuple-element.59.held), custom_call_target="tpu_custom_call", output_to_operand_aliasing={{0}: (3, {})} | custom-call | tf_op jit(solution)/shard_map/apply_tick1/pallas_call | solution.py:450
  96.6 0.7 copy-done.6
  97.2 3.5 %apply_tick2.1 = (bf16[8,192,512]{2,1,0:T(8,128)(2,1)}, bf16[3,512,512]{2,1,0:T(8,128)(2,1)}) custom-call(f32[8,128]{1,0:T(8,128)S(1)} %copy-done.6, f32[3,512,512]{2,1,0:T(8,128)} %bitcast.6, bf16[3,512,512]{2,1,0:T(8,128)(2,1)S(1)} %collective-permute-done.5.from_core, ...), custom_call_target="tpu_custom_call", output_to_operand_aliasing={{0}: (7, {})} | custom-call | tf_op jit(solution)/shard_map/apply_tick2/pallas_call | solution.py:487
  100.8 15.6 %all-to-all-start.2 = ((bf16[8,192,512]{2,1,0:T(8,128)(2,1)}), bf16[8,192,512]{2,1,0:T(8,128)(2,1)S(1)}, u32[]{:S(2)}, u32[]{:S(2)}) async-start(bf16[8,192,512]{2,1,0:T(8,128)(2,1)} %get-tuple-element.70), calls=%async_computation.2 | async-start | bytes 3145728 | tf_op jit(solution)/shard_map/all_to_all | solution.py:511
  116.4 4.5 %update_tick2.1 = f32[3,512,512]{2,1,0:T(8,128)} custom-call(bf16[3,512,512]{2,1,0:T(8,128)(2,1)S(1)} %copy-done.2, bf16[8,320,512]{2,1,0:T(8,128)(2,1)} %all-to-all-done.1.received, bf16[8,272,512]{2,1,0:T(8,128)(2,1)} %copy-done.7), custom_call_target="tpu_custom_call" | custom-call | tf_op jit(solution)/shard_map/update_tick2/pallas_call | solution.py:380
  120.9 11.2 %all-to-all-done.2.received = bf16[8,192,512]{2,1,0:T(8,128)(2,1)S(1)} async-done(((bf16[8,192,512]{2,1,0:T(8,128)(2,1)}), bf16[8,192,512]{2,1,0:T(8,128)(2,1)S(1)}, u32[]{:S(2)}, u32[]{:S(2)}) %all-to-all-start.2) | async-done | bytes 1572896 | tf_op jit(solution)/shard_map/all_to_all | solution.py:511
  132.1 1.2 copy-done.8
  133.3 2.4 %unpack_outputs.1 = bf16[3,64,4096]{2,1,0:T(8,128)(2,1)} custom-call(bf16[8,192,512]{2,1,0:T(8,128)(2,1)} %copy-done.8), custom_call_target="tpu_custom_call" | custom-call | tf_op jit(solution)/shard_map/unpack_outputs/pallas_call | solution.py:142
  (23 shorter events, 0.1 us)
Async XLA Ops:
  4.1 32.8 %all-to-all-start = ((bf16[8,272,512]{2,1,0:T(8,128)(2,1)}), bf16[8,272,512]{2,1,0:T(8,128)(2,1)S(1)}, u32[]{:S(2)}, u32[]{:S(2)}) async-start(bf16[8,272,512]{2,1,0:T(8,128)(2,1)} %pack_first.1), calls=%async_computation | async-start | bytes 4456448 | tf_op jit(solution)/shard_map/all_to_all | solution.py:511
  37.0 1.4 %copy-start.7 = (bf16[8,272,512]{2,1,0:T(8,128)(2,1)}, bf16[8,272,512]{2,1,0:T(8,128)(2,1)S(1)}, u32[]{:S(2)}) copy-start(bf16[8,272,512]{2,1,0:T(8,128)(2,1)S(1)} %all-to-all-done.received.refs_0_.first) | copy-start | bytes 6684676
  38.3 50.9 %all-to-all-start.1 = ((bf16[8,320,512]{2,1,0:T(8,128)(2,1)}), bf16[8,320,512]{2,1,0:T(8,128)(2,1)}, u32[]{:S(2)}, u32[]{:S(2)}) async-start(bf16[8,320,512]{2,1,0:T(8,128)(2,1)} %pack_rest.1), calls=%async_computation.1 | async-start | bytes 5242880 | tf_op jit(solution)/shard_map/all_to_all | solution.py:511
  48.4 4.5 %collective-permute-start.1 = (bf16[3,512,512]{2,1,0:T(8,128)(2,1)}, bf16[3,512,512]{2,1,0:T(8,128)(2,1)S(1)}, u32[]{:S(2)}, u32[]{:S(2)}) collective-permute-start(bf16[3,512,512]{2,1,0:T(8,128)(2,1)} %get-tuple-element.38), channel_id=1, source_target_pairs={{0,8},{16,24},{32,40},{48,56},{64,72},{80,88},{96,104},{112,120},{... | collective-permute-start | bytes 4718600 | tf_op jit(solution)/shard_map/ppermute | solution.py:553
  49.8 4.0 %copy-start.9 = (bf16[512,512]{1,0:T(8,128)(2,1)S(1)}, bf16[512,512]{1,0:T(8,128)(2,1)}, u32[]{:S(2)}) copy-start(bf16[512,512]{1,0:T(8,128)(2,1)} %get-tuple-element.41) | copy-start | bytes 1572868
  49.8 5.3 %collective-permute-start = (bf16[1024,512]{1,0:T(8,128)(2,1)}, bf16[1024,512]{1,0:T(8,128)(2,1)S(1)}, u32[]{:S(2)}, u32[]{:S(2)}) collective-permute-start(bf16[1024,512]{1,0:T(8,128)(2,1)} %get-tuple-element.37), channel_id=1, source_target_pairs={{8,16},{9,17},{10,18},{11,19},{12,20},{13,21},{14,22},{15,23},{24,... | collective-permute-start | bytes 3145736 | tf_op jit(solution)/shard_map/ppermute | solution.py:556
  53.0 3.4 %collective-permute-start.4 = (bf16[1024,512]{1,0:T(8,128)(2,1)}, bf16[1024,512]{1,0:T(8,128)(2,1)S(1)}, u32[]{:S(2)}, u32[]{:S(2)}) collective-permute-start(bf16[1024,512]{1,0:T(8,128)(2,1)} %get-tuple-element.42), channel_id=1, source_target_pairs={{8,16},{9,17},{10,18},{11,19},{12,20},{13,21},{14,22},{15,23},{24,... | collective-permute-start | bytes 3145736 | tf_op jit(solution)/shard_map/ppermute | solution.py:556
  53.8 17.7 %collective-permute-start.3 = (bf16[512,512]{1,0:T(8,128)(2,1)S(1)}, bf16[512,512]{1,0:T(8,128)(2,1)S(1)}, u32[]{:S(2)}, u32[]{:S(2)}) collective-permute-start(bf16[512,512]{1,0:T(8,128)(2,1)S(1)} %copy-done.9), channel_id=1, source_target_pairs={{8,16},{24,32},{40,48},{56,64},{72,80},{88,96},{104,112},{120,128}... | collective-permute-start | bytes 1572872 | tf_op jit(solution)/shard_map/ppermute | solution.py:553
  55.1 26.7 %collective-permute-start.2 = (bf16[1024,512]{1,0:T(8,128)(2,1)S(1)}, bf16[1024,512]{1,0:T(8,128)(2,1)S(1)}, u32[]{:S(2)}, u32[]{:S(2)}) collective-permute-start(bf16[1024,512]{1,0:T(8,128)(2,1)S(1)} %collective-permute-done.refs_4_), channel_id=1, source_target_pairs={{8,64},{9,65},{10,66},{11,67},{28,68},{29,69},{30,70},{31,71},{72,... | collective-permute-start | bytes 3145736 | tf_op jit(solution)/shard_map/ppermute | solution.py:556
  56.4 40.1 %collective-permute-start.6 = (bf16[1024,512]{1,0:T(8,128)(2,1)S(1)}, bf16[1024,512]{1,0:T(8,128)(2,1)}, u32[]{:S(2)}, u32[]{:S(2)}) collective-permute-start(bf16[1024,512]{1,0:T(8,128)(2,1)S(1)} %collective-permute-done.4.straight), channel_id=1, source_target_pairs={{8,64},{9,65},{10,66},{11,67},{28,68},{29,69},{30,70},{31,71},{72,... | collective-permute-start | bytes 3145736 | tf_op jit(solution)/shard_map/ppermute | solution.py:556
  57.7 38.8 %collective-permute-start.7 = (bf16[512,512]{1,0:T(8,128)(2,1)}, bf16[512,512]{1,0:T(8,128)(2,1)}, u32[]{:S(2)}, u32[]{:S(2)}) collective-permute-start(bf16[512,512]{1,0:T(8,128)(2,1)} %get-tuple-element.51), channel_id=1, source_target_pairs={{8,16},{24,32},{40,48},{56,64},{72,80},{88,96},{104,112},{120,128}... | collective-permute-start | bytes 1572872 | tf_op jit(solution)/shard_map/ppermute | solution.py:553
  71.5 0.8 copy-start.3
  81.8 1.0 copy-start.4
  82.8 0.7 copy-start.5
  87.8 8.8 %collective-permute-start.5 = (bf16[3,512,512]{2,1,0:T(8,128)(2,1)}, bf16[3,512,512]{2,1,0:T(8,128)(2,1)S(1)}, u32[]{:S(2)}, u32[]{:S(2)}) collective-permute-start(bf16[3,512,512]{2,1,0:T(8,128)(2,1)} %get-tuple-element.49), channel_id=1, source_target_pairs={{0,8},{16,24},{32,40},{48,56},{64,72},{80,88},{96,104},{112,120},{... | collective-permute-start | bytes 4718600 | tf_op jit(solution)/shard_map/ppermute | solution.py:553
  89.2 4.2 %copy-start = (bf16[3,512,512]{2,1,0:T(8,128)(2,1)S(1)}, bf16[3,512,512]{2,1,0:T(8,128)(2,1)}, u32[]{:S(2)}) copy-start(bf16[3,512,512]{2,1,0:T(8,128)(2,1)} %get-tuple-element.52.used_odd) | copy-start | bytes 4718596
  89.2 4.2 %copy-start.1 = (bf16[3,512,512]{2,1,0:T(8,128)(2,1)S(1)}, bf16[3,512,512]{2,1,0:T(8,128)(2,1)}, u32[]{:S(2)}) copy-start(bf16[3,512,512]{2,1,0:T(8,128)(2,1)} %get-tuple-element.53.used_even) | copy-start | bytes 4718596
  96.6 0.7 copy-start.6
  100.8 15.6 %copy-start.2 = (bf16[3,512,512]{2,1,0:T(8,128)(2,1)S(1)}, bf16[3,512,512]{2,1,0:T(8,128)(2,1)}, u32[]{:S(2)}) copy-start(bf16[3,512,512]{2,1,0:T(8,128)(2,1)} %get-tuple-element.71.used) | copy-start | bytes 4718596
  100.8 31.3 %all-to-all-start.2 = ((bf16[8,192,512]{2,1,0:T(8,128)(2,1)}), bf16[8,192,512]{2,1,0:T(8,128)(2,1)S(1)}, u32[]{:S(2)}, u32[]{:S(2)}) async-start(bf16[8,192,512]{2,1,0:T(8,128)(2,1)} %get-tuple-element.70), calls=%async_computation.2 | async-start | bytes 3145728 | tf_op jit(solution)/shard_map/all_to_all | solution.py:511
  132.1 1.2 copy-start.8

commit v3 on v2

--- a/solution.py
+++ b/solution.py
@@ -149,6 +149,7 @@
             pltpu.SemaphoreType.DMA((3 * HEADS,)),
             pltpu.SemaphoreType.DMA((3,)),
         ],
+        compiler_params=pltpu.CompilerParams(vmem_limit_bytes=8 * MIB),
         cost_estimate=FREE,
         name="unpack_outputs",
     )(received)
@@ -273,7 +274,7 @@
             pltpu.SemaphoreType.DMA((6,)),
             pltpu.SemaphoreType.DMA((3,)),
         ],
-        compiler_params=pltpu.CompilerParams(vmem_limit_bytes=40 * MIB),
+        compiler_params=pltpu.CompilerParams(vmem_limit_bytes=24 * MIB),
         cost_estimate=FREE,
         name="update_start",
     )(start, received)
@@ -354,7 +355,7 @@
             pltpu.SemaphoreType.DMA((6,)),
             pltpu.SemaphoreType.DMA((2,)),
         ],
-        compiler_params=pltpu.CompilerParams(vmem_limit_bytes=40 * MIB),
+        compiler_params=pltpu.CompilerParams(vmem_limit_bytes=24 * MIB),
         cost_estimate=FREE,
         name="update_tick1_%s" % ("odd" if cores else "even"),
     )(*operands)
@@ -391,7 +392,7 @@
             pltpu.SemaphoreType.DMA((6,)),
             pltpu.SemaphoreType.DMA((3,)),
         ],
-        compiler_params=pltpu.CompilerParams(vmem_limit_bytes=40 * MIB),
+        compiler_params=pltpu.CompilerParams(vmem_limit_bytes=24 * MIB),
         cost_estimate=FREE,
         name="update_tick2",
     )(used, received, first)
@@ -407,62 +408,50 @@
         produced[sources, :, :] = dot(hidden, rounded[2]).astype(BF16).reshape(4, ROWS, WIDTH)
 
 
-def first_apply(start, received, out, _, query, wide, rounded, produced, sems):
-    copies = run_copies([(start, wide), (received.at[:, slot(0), :], query)], sems)
-    copies[0].wait()
-    rounded[...] = wide[...].astype(BF16)
-    copies[1].wait()
-    apply_weights(rounded, query, produced)
-    wait_all(run_copies([(produced, out.at[:, slot(0), :])], sems))
-
-
-def apply_first(start, received):
-    return pl.pallas_call(
-        first_apply,
+def early_apply(start, used_odd, used_even, received, out, _, query, wide, rounded, produced, loads):
+    queries = run_copies([(received.at[:, slot(tick), :], query.at[tick]) for tick in range(2)], loads)
+    odd = is_odd()
+    even = jnp.logical_not(odd)
+    later = [pltpu.make_async_copy(source, rounded.at[1], loads.at[2]) for source in (used_even, used_odd)]
+    pl.when(even)(later[0].start)
+    pl.when(odd)(later[1].start)
+    first = pltpu.make_async_copy(start, wide, loads.at[3])
+    first.start()
+    stores = []
+
+    def finish(tick):
+        queries[tick].wait()
+        apply_weights(rounded.at[tick], query.at[tick], produced.at[tick])
+        store = pltpu.make_async_copy(produced.at[tick], out.at[:, slot(tick), :], loads.at[tick])
+        store.start()
+        stores.append(store)
+
+    pl.when(even)(later[0].wait)
+    pl.when(odd)(later[1].wait)
+    finish(1)
+    first.wait()
+    rounded[0] = wide[...].astype(BF16)
+    finish(0)
+    wait_all(stores)
+
+
+def apply_early(*operands):
+    return pl.pallas_call(
+        early_apply,
         out_shape=(pltpu.HBM((HEADS, 3 * ROWS, WIDTH), BF16), TOKEN),
-        in_specs=[ANY] * 2,
+        in_specs=[ANY] * len(operands),
         out_specs=(HBM, HBM),
         scratch_shapes=[
-            pltpu.VMEM((HEADS, ROWS, WIDTH), BF16),
+            pltpu.VMEM((2, HEADS, ROWS, WIDTH), BF16),
             pltpu.VMEM(STACK, F32),
-            pltpu.VMEM(STACK, BF16),
-            pltpu.VMEM((HEADS, ROWS, WIDTH), BF16),
-            pltpu.SemaphoreType.DMA((2,)),
-        ],
-        compiler_params=pltpu.CompilerParams(vmem_limit_bytes=40 * MIB),
-        cost_estimate=FREE,
-        name="apply_tick0",
-    )(start, received)
-
-
-def middle_apply(used_odd, used_even, received, held, out, _, query, rounded, produced, sems):
-    del held
-    copies = run_copies([(received.at[:, slot(1), :], query)], sems)
-    odd = is_odd()
-    pl.when(odd)(lambda: fetch_own(used_odd, rounded, sems.at[pl.ds(1, 1)]))
-    pl.when(jnp.logical_not(odd))(lambda: fetch_own(used_even, rounded, sems.at[pl.ds(1, 1)]))
-    wait_all(copies)
-    apply_weights(rounded, query, produced)
-    wait_all(run_copies([(produced, out.at[:, slot(1), :])], sems))
-
-
-def apply_middle(used_odd, used_even, received, held):
-    return pl.pallas_call(
-        middle_apply,
-        out_shape=(pltpu.HBM((HEADS, 3 * ROWS, WIDTH), BF16), TOKEN),
-        in_specs=[ANY] * 4,
-        out_specs=(HBM, HBM),
-        input_output_aliases={3: 0},
-        scratch_shapes=[
-            pltpu.VMEM((HEADS, ROWS, WIDTH), BF16),
-            pltpu.VMEM(STACK, BF16),
-            pltpu.VMEM((HEADS, ROWS, WIDTH), BF16),
-            pltpu.SemaphoreType.DMA((2,)),
-        ],
-        compiler_params=pltpu.CompilerParams(vmem_limit_bytes=40 * MIB),
-        cost_estimate=FREE,
-        name="apply_tick1",
-    )(used_odd, used_even, received, held)
+            pltpu.VMEM((2, *STACK), BF16),
+            pltpu.VMEM((2, HEADS, ROWS, WIDTH), BF16),
+            pltpu.SemaphoreType.DMA((4,)),
+        ],
+        compiler_params=pltpu.CompilerParams(vmem_limit_bytes=24 * MIB),
+        cost_estimate=FREE,
+        name="apply_ticks01",
+    )(*operands)
 
 
 def late_apply(token, start, from_core, direct, straight, relayed, received, held, out, used, query, rounded, produced, sems, load):
@@ -497,7 +486,7 @@
             pltpu.SemaphoreType.DMA((2,)),
             pltpu.SemaphoreType.DMA((6,)),
         ],
-        compiler_params=pltpu.CompilerParams(vmem_limit_bytes=40 * MIB),
+        compiler_params=pltpu.CompilerParams(vmem_limit_bytes=24 * MIB),
         cost_estimate=FREE,
         name="apply_tick2",
     )(*operands)
@@ -556,7 +545,7 @@
         return lax.ppermute(block, ("tm", "head"), route)
 
     first_sent = send_first(key_rows, value_rows, jnp.swapaxes(step_rates, 1, 2))
-    first = in_hbm(exchange(first_sent))
+    first = exchange(first_sent)
     query_rows, key_rows, value_rows, first_sent = after(query_rows, key_rows, value_rows, first_sent)
     second_sent = send_rest(query_rows, key_rows, value_rows)
     second = in_hbm(exchange(second_sent))
@@ -574,17 +563,16 @@
     relayed2 = relay(straight2, onward)
     direct1, token = after(direct1, token)
     relayed1, token = after(relayed1, mark(token, token, 6 * 10**9))
-    used_even, stacked, token = update_middle(0, first, token, [start, direct1, straight1, relayed1])
+    used_even, stacked, token = update_middle(0, first, in_hbm(token), [start, direct1, straight1, relayed1])
     core2 = shift(stacked, to_core)
     second, token = after(second, token)
-    held, _ = apply_first(start, second)
-    held, early = apply_middle(used_odd, used_even, second, held)
+    held, early = apply_early(start, in_hbm(used_odd), in_hbm(used_even), second)
     direct2, early, token = after(direct2, early, token)
     relayed2, token = after(relayed2, mark(token, early, 3 * 10**9))
     core2, token = after(core2, mark(token, token, 12 * 10**9))
-    held, used2 = apply_late(token, start, core2, [direct2, straight2, relayed2], second, held)
+    held, used2 = apply_late(in_hbm(token), start, core2, [direct2, straight2, relayed2], second, held)
     returned = exchange(held)
-    final = update_last(used2, second, first)
+    final = update_last(in_hbm(used2), second, first)
     result = place_outputs(returned)
     return result, final[None, None]
 

time: 138 us -> 133 us (0.964); the launches traced: 136 us -> 132 us
  local copies, waits for them, and re-layouts: 5.8 us -> 1.83 us
  starting transfers between devices: 35.9 us -> 37.8 us
  Pallas kernels: 33.7 us -> 31.9 us
    unnamed x20 -> x6, local copies, waits for them, and re-layouts: 5.8 us -> 1.83 us
    pallas_call x2 -> x1, Pallas kernels: 7.25 us -> 5 us  [apply_early(): pl.pallas_call(early_apply, out_shape=(pltpu.HBM((HEADS, 3 * ROWS, WIDTH)...]
    all_to_all x3, waiting for transfers between devices: 35.2 us -> 36.7 us  [exchange(): lax.all_to_all(block, 'head', split_axis=0, concat_axis=0, tiled=True)]
  transfers between devices with their start and end apart: 11 -> 11, of which waited for: 5 -> 5; matrix products, arithmetic and copies ran while one was open for 0% -> 0% of each run, Pallas kernels for 18% -> 17%
where the time goes in v3:
time: 133 us; the launch traced here: 132 us
  waiting for transfers between devices  60.1 us (45%)
  starting transfers between devices  37.8 us (28%)
  Pallas kernels  31.9 us (24%)
  local copies, waits for them, and re-layouts  1.83 us (1%)
    all_to_all x3, waiting for transfers between devices, exchange(): lax.all_to_all(block, 'head', split_axis=0, concat_axis=0, tiled=True)  36.7 us
    all_to_all x3, starting transfers between devices, exchange(): lax.all_to_all(block, 'head', split_axis=0, concat_axis=0, tiled=True)  26.2 us
    ppermute x4, waiting for transfers between devices, shift(): return lax.ppermute(block, 'tm', route)  13.7 us
    ppermute x4, waiting for transfers between devices, relay(): return lax.ppermute(block, ('tm', 'head'), route)  9.8 us
    ppermute x4, starting transfers between devices, shift(): return lax.ppermute(block, 'tm', route)  6.46 us
    pallas_call x1, Pallas kernels, update_start(): pl.pallas_call(start_update, out_shape=tuple((pltpu.HBM(shape, BF16) for...  5.11 us
    ppermute x4, starting transfers between devices, relay(): return lax.ppermute(block, ('tm', 'head'), route)  5.08 us
    pallas_call x1, Pallas kernels, apply_early(): pl.pallas_call(early_apply, out_shape=(pltpu.HBM((HEADS, 3 * ROWS, WIDTH)...  5 us
  transfers between devices with their start and end apart: 11, of which 5 were waited for; matrix products, arithmetic and copies ran while one was open for 0% of the time, Pallas kernels for 17%

profile of v3, /device:TPU:160, one launch (start us, length us, event | category | flops | bytes accessed | tf_op | source)
XLA Modules:
  0.0 132.4 jit_solution(1234959070972517134)
XLA Ops:
  0.6 3.4 %pack_first.1 = bf16[8,272,512]{2,1,0:T(8,128)(2,1)} custom-call(bf16[3,64,4096]{2,1,0:T(8,128)(2,1)} %keys.2, bf16[3,64,4096]{2,1,0:T(8,128)(2,1)} %values.2, bf16[3,24,64]{2,1,0:T(8,128)(2,1)} %bitcast.8), custom_call_target="tpu_custom_call" | custom-call | tf_op jit(solution)/shard_map/pack_first/pallas_call | solution.py:75
  4.1 5.9 %all-to-all-start = ((bf16[8,272,512]{2,1,0:T(8,128)(2,1)}), bf16[8,272,512]{2,1,0:T(8,128)(2,1)S(1)}, u32[]{:S(2)}, u32[]{:S(2)}) async-start(bf16[8,272,512]{2,1,0:T(8,128)(2,1)} %pack_first.1), calls=%async_computation | async-start | bytes 4456448 | tf_op jit(solution)/shard_map/all_to_all | solution.py:500
  10.0 2.9 %pack_rest.1 = bf16[8,320,512]{2,1,0:T(8,128)(2,1)} custom-call(bf16[3,64,4096]{2,1,0:T(8,128)(2,1)} %queries, bf16[3,64,4096]{2,1,0:T(8,128)(2,1)} %keys.2, bf16[3,64,4096]{2,1,0:T(8,128)(2,1)} %values.2), custom_call_target="tpu_custom_call" | custom-call | tf_op jit(solution)/shard_map/pack_rest/pallas_call | solution.py:104
  12.9 24.0 %all-to-all-done.received.refs_0_.first = bf16[8,272,512]{2,1,0:T(8,128)(2,1)S(1)} async-done(((bf16[8,272,512]{2,1,0:T(8,128)(2,1)}), bf16[8,272,512]{2,1,0:T(8,128)(2,1)S(1)}, u32[]{:S(2)}, u32[]{:S(2)}) %all-to-all-start) | async-done | bytes 2228256 | tf_op jit(solution)/shard_map/all_to_all | solution.py:500
  36.9 4.9 %all-to-all-start.1 = ((bf16[8,320,512]{2,1,0:T(8,128)(2,1)}), bf16[8,320,512]{2,1,0:T(8,128)(2,1)}, u32[]{:S(2)}, u32[]{:S(2)}) async-start(bf16[8,320,512]{2,1,0:T(8,128)(2,1)} %pack_rest.1), calls=%async_computation.1 | async-start | bytes 5242880 | tf_op jit(solution)/shard_map/all_to_all | solution.py:500
  41.8 5.1 %update_start.1 = (bf16[3,512,512]{2,1,0:T(8,128)(2,1)}, bf16[512,512]{1,0:T(8,128)(2,1)}, bf16[1024,512]{1,0:T(8,128)(2,1)}) custom-call(f32[3,512,512]{2,1,0:T(8,128)} %bitcast.3, bf16[8,272,512]{2,1,0:T(8,128)(2,1)S(1)} %all-to-all-done.received.refs_0_.first), custom_call_target="tpu_custom_call" | custom-call | tf_op jit(solution)/shard_map/update_start/pallas_call | solution.py:262
  46.9 1.4 %collective-permute-start.1 = (bf16[3,512,512]{2,1,0:T(8,128)(2,1)}, bf16[3,512,512]{2,1,0:T(8,128)(2,1)S(1)}, u32[]{:S(2)}, u32[]{:S(2)}) collective-permute-start(bf16[3,512,512]{2,1,0:T(8,128)(2,1)} %get-tuple-element.37), channel_id=1, source_target_pairs={{0,8},{16,24},{32,40},{48,56},{64,72},{80,88},{96,104},{112,120},{... | collective-permute-start | bytes 4718600 | tf_op jit(solution)/shard_map/ppermute | solution.py:542
  48.3 0.9 collective-permute-start
  49.2 2.3 %collective-permute-done.1.refs_1_ = bf16[3,512,512]{2,1,0:T(8,128)(2,1)S(1)} collective-permute-done((bf16[3,512,512]{2,1,0:T(8,128)(2,1)}, bf16[3,512,512]{2,1,0:T(8,128)(2,1)S(1)}, u32[]{:S(2)}, u32[]{:S(2)}) %collective-permute-start.1) | collective-permute-done | bytes 1572896 | tf_op jit(solution)/shard_map/ppermute | solution.py:542
  51.4 0.1 update_tick1_odd.1
  51.5 1.6 %collective-permute-start.4 = (bf16[1024,512]{1,0:T(8,128)(2,1)}, bf16[1024,512]{1,0:T(8,128)(2,1)}, u32[]{:S(2)}, u32[]{:S(2)}) collective-permute-start(bf16[1024,512]{1,0:T(8,128)(2,1)} %get-tuple-element.41), channel_id=1, source_target_pairs={{8,16},{9,17},{10,18},{11,19},{12,20},{13,21},{14,22},{15,23},{24,... | collective-permute-start | bytes 3145736 | tf_op jit(solution)/shard_map/ppermute | solution.py:545
  53.2 1.3 collective-permute-start.3
  54.5 0.0 collective-permute-done.refs_4_
  54.5 1.3 collective-permute-start.2
  55.8 0.0 collective-permute-done.4.straight
  55.8 1.3 collective-permute-start.6
  57.1 1.3 collective-permute-start.7
  58.4 11.4 %collective-permute-done.3.refs_3_ = bf16[512,512]{1,0:T(8,128)(2,1)S(1)} collective-permute-done((bf16[512,512]{1,0:T(8,128)(2,1)S(1)}, bf16[512,512]{1,0:T(8,128)(2,1)S(1)}, u32[]{:S(2)}, u32[]{:S(2)}) %collective-permute-start.3) | collective-permute-done | bytes 524320 | tf_op jit(solution)/shard_map/ppermute | solution.py:542
  69.8 0.8 copy-done
  70.6 9.8 %collective-permute-done.2.refs_5_ = bf16[1024,512]{1,0:T(8,128)(2,1)} collective-permute-done((bf16[1024,512]{1,0:T(8,128)(2,1)S(1)}, bf16[1024,512]{1,0:T(8,128)(2,1)}, u32[]{:S(2)}, u32[]{:S(2)}) %collective-permute-start.2) | collective-permute-done | bytes 1048608 | tf_op jit(solution)/shard_map/ppermute | solution.py:545
  80.4 1.0 copy-done.1
  81.4 4.4 %update_tick1_even.1 = (bf16[3,512,512]{2,1,0:T(8,128)(2,1)}, bf16[3,512,512]{2,1,0:T(8,128)(2,1)}, f32[8,128]{1,0:T(8,128)}) custom-call(bf16[8,272,512]{2,1,0:T(8,128)(2,1)S(1)} %all-to-all-done.received.refs_0_.first, f32[8,128]{1,0:T(8,128)} %mark.3.refs_1_, f32[3,512,512]{2,1,0:T(8,128)} %bitcast.4, bf16[512,512]{1,0:T(8,128)(2,1)S(1)} %copy-done.1, ...), custom_call_target="tpu_custom_call" | custom-call | tf_op jit(solution)/shard_map/update_tick1_even/pallas_call | solution.py:343
  85.8 2.5 %collective-permute-start.5 = (bf16[3,512,512]{2,1,0:T(8,128)(2,1)}, bf16[3,512,512]{2,1,0:T(8,128)(2,1)}, u32[]{:S(2)}, u32[]{:S(2)}) collective-permute-start(bf16[3,512,512]{2,1,0:T(8,128)(2,1)} %get-tuple-element.48), channel_id=1, source_target_pairs={{0,8},{16,24},{32,40},{48,56},{64,72},{80,88},{96,104},{112,120},{... | collective-permute-start | bytes 4718600 | tf_op jit(solution)/shard_map/ppermute | solution.py:542
  88.3 5.0 %apply_ticks01.1 = (bf16[8,192,512]{2,1,0:T(8,128)(2,1)}, f32[8,128]{1,0:T(8,128)}) custom-call(f32[3,512,512]{2,1,0:T(8,128)} %bitcast.5, bf16[3,512,512]{2,1,0:T(8,128)(2,1)} %get-tuple-element.51.used_odd, bf16[3,512,512]{2,1,0:T(8,128)(2,1)} %get-tuple-element.52.used_even, bf16[8,320,512]{2,1,0:T(8,128)(2,1)} %all-to-all-done.1.received), custom_call_target="tpu_custom_call" | custom-call | tf_op jit(solution)/shard_map/apply_ticks01/pallas_call | solution.py:439
  93.3 0.0 collective-permute-done.7.direct
  93.3 0.0 collective-permute-done.6.relayed
  93.4 0.0 collective-permute-done.5.from_core
  93.4 3.5 %apply_tick2.1 = (bf16[8,192,512]{2,1,0:T(8,128)(2,1)}, bf16[3,512,512]{2,1,0:T(8,128)(2,1)}) custom-call(f32[8,128]{1,0:T(8,128)} %mark.5.token, f32[3,512,512]{2,1,0:T(8,128)} %bitcast.6, bf16[3,512,512]{2,1,0:T(8,128)(2,1)} %collective-permute-done.5.from_core, bf16[512,512]{1,0:T(8,128)(2,1)} %collective-permute-done.7.direct, ...), custom_call_target="tpu_custom_call", output_to_operand_aliasing={{0}: (7, {})} | custom-call | tf_op jit(solution)/shard_map/apply_tick2/pallas_call | solution.py:476
  96.9 15.4 %all-to-all-start.2 = ((bf16[8,192,512]{2,1,0:T(8,128)(2,1)}), bf16[8,192,512]{2,1,0:T(8,128)(2,1)}, u32[]{:S(2)}, u32[]{:S(2)}) async-start(bf16[8,192,512]{2,1,0:T(8,128)(2,1)} %get-tuple-element.68), calls=%async_computation.2 | async-start | bytes 3145728 | tf_op jit(solution)/shard_map/all_to_all | solution.py:500
  112.3 5.0 %update_tick2.1 = f32[3,512,512]{2,1,0:T(8,128)} custom-call(bf16[3,512,512]{2,1,0:T(8,128)(2,1)} %get-tuple-element.69.used, bf16[8,320,512]{2,1,0:T(8,128)(2,1)} %all-to-all-done.1.received, bf16[8,272,512]{2,1,0:T(8,128)(2,1)S(1)} %all-to-all-done.received.refs_0_.first), custom_call_target="tpu_custom_call" | custom-call | tf_op jit(solution)/shard_map/update_tick2/pallas_call | solution.py:381
  117.3 12.7 %all-to-all-done.2.received = bf16[8,192,512]{2,1,0:T(8,128)(2,1)} async-done(((bf16[8,192,512]{2,1,0:T(8,128)(2,1)}), bf16[8,192,512]{2,1,0:T(8,128)(2,1)}, u32[]{:S(2)}, u32[]{:S(2)}) %all-to-all-start.2) | async-done | bytes 1572896 | tf_op jit(solution)/shard_map/all_to_all | solution.py:500
  130.0 2.4 %unpack_outputs.1 = bf16[3,64,4096]{2,1,0:T(8,128)(2,1)} custom-call(bf16[8,192,512]{2,1,0:T(8,128)(2,1)} %all-to-all-done.2.received), custom_call_target="tpu_custom_call" | custom-call | tf_op jit(solution)/shard_map/unpack_outputs/pallas_call | solution.py:142
  (8 shorter events, 0.0 us)
Async XLA Ops:
  4.1 32.8 %all-to-all-start = ((bf16[8,272,512]{2,1,0:T(8,128)(2,1)}), bf16[8,272,512]{2,1,0:T(8,128)(2,1)S(1)}, u32[]{:S(2)}, u32[]{:S(2)}) async-start(bf16[8,272,512]{2,1,0:T(8,128)(2,1)} %pack_first.1), calls=%async_computation | async-start | bytes 4456448 | tf_op jit(solution)/shard_map/all_to_all | solution.py:500
  36.9 51.4 %all-to-all-start.1 = ((bf16[8,320,512]{2,1,0:T(8,128)(2,1)}), bf16[8,320,512]{2,1,0:T(8,128)(2,1)}, u32[]{:S(2)}, u32[]{:S(2)}) async-start(bf16[8,320,512]{2,1,0:T(8,128)(2,1)} %pack_rest.1), calls=%async_computation.1 | async-start | bytes 5242880 | tf_op jit(solution)/shard_map/all_to_all | solution.py:500
  46.9 4.5 %collective-permute-start.1 = (bf16[3,512,512]{2,1,0:T(8,128)(2,1)}, bf16[3,512,512]{2,1,0:T(8,128)(2,1)S(1)}, u32[]{:S(2)}, u32[]{:S(2)}) collective-permute-start(bf16[3,512,512]{2,1,0:T(8,128)(2,1)} %get-tuple-element.37), channel_id=1, source_target_pairs={{0,8},{16,24},{32,40},{48,56},{64,72},{80,88},{96,104},{112,120},{... | collective-permute-start | bytes 4718600 | tf_op jit(solution)/shard_map/ppermute | solution.py:542
  48.3 4.9 %copy-start.2 = (bf16[512,512]{1,0:T(8,128)(2,1)S(1)}, bf16[512,512]{1,0:T(8,128)(2,1)}, u32[]{:S(2)}) copy-start(bf16[512,512]{1,0:T(8,128)(2,1)} %get-tuple-element.40) | copy-start | bytes 1572868
  48.3 6.2 %collective-permute-start = (bf16[1024,512]{1,0:T(8,128)(2,1)}, bf16[1024,512]{1,0:T(8,128)(2,1)S(1)}, u32[]{:S(2)}, u32[]{:S(2)}) collective-permute-start(bf16[1024,512]{1,0:T(8,128)(2,1)} %get-tuple-element.36), channel_id=1, source_target_pairs={{8,16},{9,17},{10,18},{11,19},{12,20},{13,21},{14,22},{15,23},{24,... | collective-permute-start | bytes 3145736 | tf_op jit(solution)/shard_map/ppermute | solution.py:545
  51.5 4.2 %collective-permute-start.4 = (bf16[1024,512]{1,0:T(8,128)(2,1)}, bf16[1024,512]{1,0:T(8,128)(2,1)}, u32[]{:S(2)}, u32[]{:S(2)}) collective-permute-start(bf16[1024,512]{1,0:T(8,128)(2,1)} %get-tuple-element.41), channel_id=1, source_target_pairs={{8,16},{9,17},{10,18},{11,19},{12,20},{13,21},{14,22},{15,23},{24,... | collective-permute-start | bytes 3145736 | tf_op jit(solution)/shard_map/ppermute | solution.py:545
  53.2 16.6 %collective-permute-start.3 = (bf16[512,512]{1,0:T(8,128)(2,1)S(1)}, bf16[512,512]{1,0:T(8,128)(2,1)S(1)}, u32[]{:S(2)}, u32[]{:S(2)}) collective-permute-start(bf16[512,512]{1,0:T(8,128)(2,1)S(1)} %copy-done.2), channel_id=1, source_target_pairs={{8,16},{24,32},{40,48},{56,64},{72,80},{88,96},{104,112},{120,128}... | collective-permute-start | bytes 1572872 | tf_op jit(solution)/shard_map/ppermute | solution.py:542
  54.5 25.9 %collective-permute-start.2 = (bf16[1024,512]{1,0:T(8,128)(2,1)S(1)}, bf16[1024,512]{1,0:T(8,128)(2,1)}, u32[]{:S(2)}, u32[]{:S(2)}) collective-permute-start(bf16[1024,512]{1,0:T(8,128)(2,1)S(1)} %collective-permute-done.refs_4_), channel_id=1, source_target_pairs={{8,64},{9,65},{10,66},{11,67},{28,68},{29,69},{30,70},{31,71},{72,... | collective-permute-start | bytes 3145736 | tf_op jit(solution)/shard_map/ppermute | solution.py:545
  55.8 37.5 %collective-permute-start.6 = (bf16[1024,512]{1,0:T(8,128)(2,1)}, bf16[1024,512]{1,0:T(8,128)(2,1)}, u32[]{:S(2)}, u32[]{:S(2)}) collective-permute-start(bf16[1024,512]{1,0:T(8,128)(2,1)} %collective-permute-done.4.straight), channel_id=1, source_target_pairs={{8,64},{9,65},{10,66},{11,67},{28,68},{29,69},{30,70},{31,71},{72,... | collective-permute-start | bytes 3145736 | tf_op jit(solution)/shard_map/ppermute | solution.py:545
  57.1 36.2 %collective-permute-start.7 = (bf16[512,512]{1,0:T(8,128)(2,1)}, bf16[512,512]{1,0:T(8,128)(2,1)}, u32[]{:S(2)}, u32[]{:S(2)}) collective-permute-start(bf16[512,512]{1,0:T(8,128)(2,1)} %get-tuple-element.50), channel_id=1, source_target_pairs={{8,16},{24,32},{40,48},{56,64},{72,80},{88,96},{104,112},{120,128}... | collective-permute-start | bytes 1572872 | tf_op jit(solution)/shard_map/ppermute | solution.py:542
  69.8 0.8 copy-start
  80.4 1.0 copy-start.1
  85.8 7.6 %collective-permute-start.5 = (bf16[3,512,512]{2,1,0:T(8,128)(2,1)}, bf16[3,512,512]{2,1,0:T(8,128)(2,1)}, u32[]{:S(2)}, u32[]{:S(2)}) collective-permute-start(bf16[3,512,512]{2,1,0:T(8,128)(2,1)} %get-tuple-element.48), channel_id=1, source_target_pairs={{0,8},{16,24},{32,40},{48,56},{64,72},{80,88},{96,104},{112,120},{... | collective-permute-start | bytes 4718600 | tf_op jit(solution)/shard_map/ppermute | solution.py:542
  96.9 33.1 %all-to-all-start.2 = ((bf16[8,192,512]{2,1,0:T(8,128)(2,1)}), bf16[8,192,512]{2,1,0:T(8,128)(2,1)}, u32[]{:S(2)}, u32[]{:S(2)}) async-start(bf16[8,192,512]{2,1,0:T(8,128)(2,1)} %get-tuple-element.68), calls=%async_computation.2 | async-start | bytes 3145728 | tf_op jit(solution)/shard_map/all_to_all | solution.py:500
